TPU v7x, 32 devices: a whole 2x2x4 slice. The times are simulated.
32 devices in a mesh: row: 4 (over y, x), col: 8 (over z, core).
Axes of the slice: x: 2, y: 2, z: 4, core: 2. Of those that a mesh axis runs over, the one named last changes fastest.
Arguments:
- state: float32 [3072, 3072], P('col', 'row'), may hold values from -300 to 300
- noise: float32 [3072, 3072], P('col', 'row'), may hold values from -6 to 6
- mod_shift: float32 [3072], P('col'), may hold values from -3 to 3
- mod_scale: float32 [3072], P('col'), may hold values from -2.5 to 2.5
- mod_gate: float32 [3072], P('col'), may hold values from 0.3 to 3
- w_in: bfloat16 [3072, 12288], P('row', 'col'), may hold values from -0.109375 to 0.109375
- b_in: float32 [12288], P('col'), may hold values from -3 to 3
- w_out: bfloat16 [3072, 12288], P('col', 'row'), may hold values from -0.0546875 to 0.0546875
- b_out: float32 [3072], P('col'), may hold values from -2.5 to 2.5
Outputs:
- purified: float32 [3072, 3072], P('col', 'row')
- predicted: float32 [3072, 3072], P('col', 'row')
All inputs are finite; a program needn't handle non-finite values.
Results may differ from a plain program's by a relative error of at most 0.00049.
Values may be sent and summed in bfloat16 or wider, within the bound.
A program may use at most 128 MiB of HBM per device.

v0:
```python
import math

import jax
import jax.numpy as jnp
from jax import lax
from jax.sharding import PartitionSpec as P

D = 3072


beta_now = 2.09
step_width = 0.02
sigma_now = 0.322


def on_device(state, noise, mod_shift, mod_scale, mod_gate, w_in, b_in, w_out, b_out):
    w_in_all = lax.all_gather(w_in, "row", axis=0, tiled=True)
    w_out_all = lax.all_gather(w_out, "row", axis=1, tiled=True)
    col_sums, squares = lax.psum((jnp.sum(state, axis=0), jnp.sum(state * state, axis=0)), "col")
    center = col_sums / D
    spread = squares / D - center * center
    normed = (
        (state - center[None, :]) * lax.rsqrt(spread[None, :] + 1e-06) * (1.0 + mod_scale[:, None])
        + mod_shift[:, None]
    ).astype(jnp.bfloat16)
    normed_all = lax.all_gather(normed, "col", axis=0, tiled=True)
    pre_act = lax.dot_general(
        w_in_all, normed_all, (((0,), (0,)), ((), ())), preferred_element_type=jnp.float32
    )
    hidden = jax.nn.gelu(pre_act + b_in[:, None], approximate=True).astype(jnp.bfloat16)
    hidden_all = lax.all_gather(hidden, "col", axis=0, tiled=True)
    mixed_out = jnp.dot(w_out_all, hidden_all, preferred_element_type=jnp.float32)
    branch = mixed_out + b_out[:, None]
    predicted = state + mod_gate[:, None] * branch
    purified = (
        state * (1.0 + 0.5 * beta_now * step_width)
        - beta_now * step_width / sigma_now * predicted
        + math.sqrt(beta_now * step_width) * noise
    )
    return (purified, predicted)


def solution(mesh):
    in_specs = (
        P("col", "row"),
        P("col", "row"),
        P("col"),
        P("col"),
        P("col"),
        P("row", "col"),
        P("col"),
        P("col", "row"),
        P("col"),
    )
    out_specs = (P("col", "row"), P("col", "row"))
    return jax.shard_map(
        on_device, mesh=mesh, in_specs=in_specs, out_specs=out_specs, check_vma=False
    )
```

profile of v0, /device:TPU:0, one launch (start us, length us, event | category | flops | bytes accessed | tf_op | source)
XLA Modules:
  0.0 473.4 jit_solution(9994325539912814488)
XLA Ops:
  7.2 0.0 all-gather.5.cloned.1.call-start
  7.2 0.7 broadcast_add_fusion
  7.9 1.4 fusion.11
  9.3 18.3 %all-reduce = (f32[768]{0:T(1024)S(1)}, f32[768]{0:T(1024)S(1)}) all-reduce(f32[768]{0:T(1024)S(1)} %get-tuple-element.5, f32[768]{0:T(1024)S(1)} %get-tuple-element.4), channel_id=1, replica_groups=mesh['row'=4,'col'=8] {'col'}, use_global_device_ids=true, to_apply=%region_3.0 | all-reduce | flops 1536 | bytes 12288 | tf_op jit(solution)/shard_map/psum | solution.py:19
  27.7 2.3 add_convert_fusion
  29.9 0.0 all-gather.5.cloned.1.call-update
  30.0 0.0 copy-start.2
  30.0 0.0 all-gather.7.cloned.1.call-start
  30.0 0.7 all-gather.7.cloned.1.call-update
  30.7 0.0 all-gather.11.cloned.1.call-start
  30.8 0.7 all-gather.11.cloned.1.call-update
  31.5 0.0 all-gather.9.cloned.1.call-start
  31.5 48.5 %all-gather.5.cloned.1.call-done = bf16[3072,768]{1,0:T(8,128)(2,1)} async-done(((bf16[384,768]{1,0:T(8,128)(2,1)}), bf16[3072,768]{1,0:T(8,128)(2,1)}) %all-gather.5.cloned.1.call-update) | async-done | bytes 4718608 | tf_op jit(solution)/shard_map/all_gather | solution.py:26
  80.1 97.0 %all-gather.7.cloned.1.call-done = bf16[3072,1536]{1,0:T(8,128)(2,1)} async-done(((bf16[768,1536]{1,0:T(8,128)(2,1)}), bf16[3072,1536]{1,0:T(8,128)(2,1)}) %all-gather.7.cloned.1.call-update) | async-done | bytes 9437200 | tf_op jit(solution)/shard_map/all_gather | solution.py:17
  177.1 0.0 copy-done.2
  177.1 13.7 %fusion.7 = bf16[1536,768]{0,1:T(8,128)(2,1)} fusion(bf16[3072,768]{1,0:T(8,128)(2,1)} %all-gather.5.cloned.1.call-done, bf16[3072,1536]{1,0:T(8,128)(2,1)} %all-gather.7.cloned.1.call-done, f32[1536]{0:T(1024)S(1)} %copy-done.2), kind=kOutput, calls=%fused_computation.8 | convolution fusion | flops 7259553792 | bytes 16521216 | tf_op jit(solution)/shard_map/dot_general | solution.py:27
  190.7 0.0 copy-start
  190.7 0.0 copy-start.1
  190.7 0.0 all-gather.9.cloned.1.call-update
  190.8 1.3 copy-done
  192.1 0.0 copy-start.3
  192.1 0.0 copy-start.4
  192.1 0.4 copy.11
  192.5 0.0 copy-done.1
  192.5 0.4 copy.13
  192.9 82.4 %all-gather.11.cloned.1.call-done = bf16[384,12288]{1,0:T(8,128)(2,1)} async-done(((bf16[384,3072]{1,0:T(8,128)(2,1)}), bf16[384,12288]{1,0:T(8,128)(2,1)}) %all-gather.11.cloned.1.call-update) | async-done | bytes 9437200 | tf_op jit(solution)/shard_map/all_gather | solution.py:18
  275.3 169.8 %all-gather.9.cloned.1.call-done = bf16[12288,768]{0,1:T(8,128)(2,1)} async-done(((bf16[1536,768]{0,1:T(8,128)(2,1)}), bf16[12288,768]{0,1:T(8,128)(2,1)}) %all-gather.9.cloned.1.call-update) | async-done | bytes 18874384 | tf_op jit(solution)/shard_map/all_gather | solution.py:31
  445.1 0.0 copy-done.3
  445.1 0.0 copy-done.4
  445.1 17.8 %multiply_add_fusion = (f32[384,768]{0,1:T(8,128)}, f32[384,768]{0,1:T(8,128)S(1)}) fusion(f32[384,768]{0,1:T(8,128)S(1)} %copy.13, f32[384,768]{0,1:T(8,128)S(1)} %copy.11, f32[384]{0:T(512)S(1)} %copy-done.3, bf16[12288,768]{0,1:T(8,128)(2,1)} %all-gather.9.cloned.1.call-done, bf16[384,12288]{1,0:T(8,128)(2,1)} %all-gather.11.cloned.1.call-done, ...), kind=kOutput, calls=%fused_computation.13 | convolution fusion | flops 7250116608 | bytes 33033216 | tf_op jit(solution)/shard_map/dot_general | solution.py:32
  462.8 2.7 copy.14
  465.5 1.4 copy.15
  (1 shorter events, 0.0 us)
Async XLA Ops:
  7.2 72.9 %all-gather.5.cloned.1.call-start = ((), (), s32[]{:S(2)}) async-start(), calls=%async_computation | async-start | bytes 5308416 | tf_op jit(solution)/shard_map/all_gather | solution.py:26
  30.0 147.1 %copy-start.2 = (f32[1536]{0:T(1024)S(1)}, f32[1536]{0:T(1024)}, u32[]{:S(2)}) copy-start(f32[1536]{0:T(1024)} %param.15) | copy-start | bytes 18436
  30.0 147.1 %all-gather.7.cloned.1.call-start = ((), (), s32[]{:S(2)}) async-start(), calls=%async_computation.1 | async-start | bytes 11796480 | tf_op jit(solution)/shard_map/all_gather | solution.py:17
  30.7 244.6 %all-gather.11.cloned.1.call-start = ((), (), s32[]{:S(2)}) async-start(), calls=%async_computation.3 | async-start | bytes 11796480 | tf_op jit(solution)/shard_map/all_gather | solution.py:18
  31.5 413.6 %all-gather.9.cloned.1.call-start = ((), (), s32[]{:S(2)}) async-start(), calls=%async_computation.2 | async-start | bytes 21233664 | tf_op jit(solution)/shard_map/all_gather | solution.py:31
  190.7 1.4 copy-start
  190.7 1.8 copy-start.1
  192.1 253.0 %copy-start.3 = (f32[384]{0:T(512)S(1)}, f32[384]{0:T(512)}, u32[]{:S(2)}) copy-start(f32[384]{0:T(512)} %param.17) | copy-start | bytes 4612
  192.1 253.0 %copy-start.4 = (f32[384]{0:T(512)S(1)}, f32[384]{0:T(512)}, u32[]{:S(2)}) copy-start(f32[384]{0:T(512)} %param.13) | copy-start | bytes 4612
Sparse Core Ops, SparseCore 0:
  30.1 49.9 all-gather.4
  81.9 95.1 all-gather.6
  178.9 96.3 all-gather.10
  276.8 168.2 all-gather.8
where the time goes:
time: 474 us; the launch traced here: 473 us
  waiting for transfers between devices  399 us (84%)
  matrix products  31.4 us (7%)
  blocking collectives  18.3 us (4%)
  between operations  13.8 us (3%)
  local copies, waits for them, and re-layouts  6.13 us (1%)
    all_gather x1, waiting for transfers between devices, on_device(): hidden_all = lax.all_gather(hidden, 'col', axis=0, tiled=True)  170 us
    all_gather x1, waiting for transfers between devices, on_device(): w_in_all = lax.all_gather(w_in, 'row', axis=0, tiled=True)  97 us
    all_gather x1, waiting for transfers between devices, on_device(): w_out_all = lax.all_gather(w_out, 'row', axis=1, tiled=True)  82.4 us
    all_gather x1, waiting for transfers between devices, on_device(): normed_all = lax.all_gather(normed, 'col', axis=0, tiled=True)  48.5 us
    psum x1, blocking collectives, on_device(): lax.psum((jnp.sum(state, axis=0), jnp.sum(state * state, axis=0)), 'col')  18.3 us
    dot_general x1, matrix products, on_device(): jnp.dot(w_out_all, hidden_all, preferred_element_type=jnp.float32)  17.8 us
    dot_general x1, matrix products, on_device(): lax.dot_general(w_in_all, normed_all, (((0,), (0,)), ((), ())), preferred...  13.7 us
  transfers between devices with their start and end apart: 4, of which 4 were waited for; matrix products, arithmetic and copies ran while one was open for 3% of the time, Pallas kernels for 0%

commit v1 on v0

v1 whole, which is shorter than its diff:
```python
import math

import jax
import jax.numpy as jnp
from jax import lax
from jax.sharding import PartitionSpec as P

D = 3072


beta_now = 2.09
step_width = 0.02
sigma_now = 0.322


def flipped(value, axis, bits):
    devices = lax.axis_size(axis)
    return lax.ppermute(value, axis, [(i, i ^ bits) for i in range(devices)])


def spread_blocks(block, dim, axis):
    half = block.shape[dim] // 2
    held = {0: block}
    pieces = {0: [(0, block)]}
    order = sorted(range(1, lax.axis_size(axis)), key=lambda k: (k.bit_count(), k))
    for k in order:
        low = k & -k
        high = 1 << (k.bit_length() - 1)
        if low == high:
            held[k] = flipped(block, axis, k)
            pieces[k] = [(0, held[k])]
        else:
            first = lax.slice_in_dim(held[k ^ low], 0, half, axis=dim)
            second = lax.slice_in_dim(held[k ^ high], half, 2 * half, axis=dim)
            first, second = flipped(first, axis, low), flipped(second, axis, high)
            pieces[k] = [(0, first), (half, second)]
            if k.bit_count() < lax.axis_size(axis).bit_length() - 1:
                held[k] = lax.concatenate([first, second], dim)
    return pieces, held


def on_device(state, noise, mod_shift, mod_scale, mod_gate, w_in, b_in, w_out, b_out):
    row = lax.axis_index("row")
    in_pieces, in_held = spread_blocks(w_in, 0, "row")
    w_out, _ = lax.optimization_barrier((w_out, in_held[1]))
    out_pieces, _ = spread_blocks(w_out, 1, "row")
    col_sums, squares = lax.psum((jnp.sum(state, axis=0), jnp.sum(state * state, axis=0)), "col")
    center = col_sums / D
    spread = squares / D - center * center
    normed = (
        (state - center[None, :]) * lax.rsqrt(spread[None, :] + 1e-06) * (1.0 + mod_scale[:, None])
        + mod_shift[:, None]
    ).astype(jnp.bfloat16)
    normed_all = lax.all_gather(normed, "col", axis=0, tiled=True)
    tokens = state.shape[1]
    chunk = tokens // 3 if tokens % 384 == 0 else tokens
    spans = [(lo, lo + chunk) for lo in range(0, tokens, chunk)]

    gathered = []
    for lo, hi in spans:
        pre_act = None
        for k, parts in in_pieces.items():
            for offset, piece in parts:
                start = (row ^ k) * w_in.shape[0] + offset
                part = lax.dynamic_slice(normed_all, (start, lo), (piece.shape[0], hi - lo))
                term = lax.dot_general(
                    piece, part, (((0,), (0,)), ((), ())), preferred_element_type=jnp.float32
                )
                pre_act = term if pre_act is None else pre_act + term
        hidden = jax.nn.gelu(pre_act + b_in[:, None], approximate=True).astype(jnp.bfloat16)
        gathered.append(lax.all_gather(hidden, "col", axis=0, tiled=True))

    outs = []
    for (lo, hi), hidden_all in zip(spans, gathered):
        mixed_out = None
        for k, parts in out_pieces.items():
            for offset, piece in parts:
                start = (row ^ k) * w_out.shape[1] + offset
                part = lax.dynamic_slice(hidden_all, (start, 0), (piece.shape[1], hi - lo))
                term = jnp.dot(piece, part, preferred_element_type=jnp.float32)
                mixed_out = term if mixed_out is None else mixed_out + term
        branch = mixed_out + b_out[:, None]
        now = state[:, lo:hi]
        predicted = now + mod_gate[:, None] * branch
        purified = (
            now * (1.0 + 0.5 * beta_now * step_width)
            - beta_now * step_width / sigma_now * predicted
            + math.sqrt(beta_now * step_width) * noise[:, lo:hi]
        )
        outs.append((purified, predicted))
    return tuple(lax.concatenate(list(parts), 1) for parts in zip(*outs))


def solution(mesh):
    in_specs = (
        P("col", "row"),
        P("col", "row"),
        P("col"),
        P("col"),
        P("col"),
        P("row", "col"),
        P("col"),
        P("col", "row"),
        P("col"),
    )
    out_specs = (P("col", "row"), P("col", "row"))
    return jax.shard_map(
        on_device, mesh=mesh, in_specs=in_specs, out_specs=out_specs, check_vma=False
    )
```

time: 474 us -> 351 us (0.74)
  waiting for transfers between devices: 399 us -> 206 us
  matrix products: 31.4 us -> 70.5 us
  local copies, waits for them, and re-layouts: 6.13 us -> 26.2 us
  starting transfers between devices: 0.16 us -> 10.4 us
    all_gather x3, waiting for transfers between devices: 349 us -> 86 us  [on_device(): gathered.append(lax.all_gather(hidden, 'col', axis=0, tiled=True))]
    ppermute x0 -> x8, waiting for transfers between devices: none -> 120 us  [flipped(): return lax.ppermute(value, axis, [(i, i ^ bits) for i in range(devices)])]
    all_gather x1, waiting for transfers between devices: 48.5 us -> 0.01 us  [on_device(): normed_all = lax.all_gather(normed, 'col', axis=0, tiled=True)]
    dot_general x2 -> x30, matrix products: 31.4 us -> 70.5 us  [the longest x15 36.3 us: on_device(): term = jnp.dot(piece, part, preferred_element_type=jnp.float32)]
    slice x0 -> x6, local copies, waits for them, and re-layouts: none -> 10.3 us  [the longest x2 3.46 us: spread_blocks(): second = lax.slice_in_dim(held[k ^ high], half, 2 * half, axis=dim)]
    ppermute x0 -> x8, starting transfers between devices: none -> 10.1 us  [flipped(): return lax.ppermute(value, axis, [(i, i ^ bits) for i in range(devices)])]
    unnamed x14 -> x56, local copies, waits for them, and re-layouts: 6.13 us -> 16 us
  transfers between devices with their start and end apart: 4 -> 12, of which waited for: 4 -> 6; matrix products, arithmetic and copies ran while one was open for 3% -> 22% of each run, Pallas kernels for 0% -> 0%
where the time goes in v1:
time: 351 us; the launch traced here: 350 us
  waiting for transfers between devices  206 us (59%)
  matrix products  70.5 us (20%)
  local copies, waits for them, and re-layouts  26.2 us (7%)
  blocking collectives  18.3 us (5%)
  between operations  14.3 us (4%)
  starting transfers between devices  10.4 us (3%)
  other arithmetic  4.1 us (1%)
    ppermute x8, waiting for transfers between devices, flipped(): return lax.ppermute(value, axis, [(i, i ^ bits) for i in range(devices)])  120 us
    all_gather x3, waiting for transfers between devices, on_device(): gathered.append(lax.all_gather(hidden, 'col', axis=0, tiled=True))  86 us
    dot_general x15, matrix products, on_device(): term = jnp.dot(piece, part, preferred_element_type=jnp.float32)  36.3 us
    dot_general x15, matrix products, on_device(): lax.dot_general(piece, part, (((0,), (0,)), ((), ())), preferred_element_...  34.1 us
    psum x1, blocking collectives, on_device(): lax.psum((jnp.sum(state, axis=0), jnp.sum(state * state, axis=0)), 'col')  18.3 us
    unnamed x56, local copies, waits for them, and re-layouts  16 us
    ppermute x8, starting transfers between devices, flipped(): return lax.ppermute(value, axis, [(i, i ^ bits) for i in range(devices)])  10.1 us
  transfers between devices with their start and end apart: 12, of which 6 were waited for; matrix products, arithmetic and copies ran while one was open for 22% of the time, Pallas kernels for 0%

profile of v1, /device:TPU:0, one launch (start us, length us, event | category | flops | bytes accessed | tf_op | source)
XLA Modules:
  0.0 349.6 jit_solution(6745905828301749824)
XLA Ops:
  7.2 0.8 broadcast_add_fusion
  8.0 1.4 fusion.183
  9.4 18.3 %all-reduce = (f32[768]{0:T(1024)S(1)}, f32[768]{0:T(1024)S(1)}) all-reduce(f32[768]{0:T(1024)S(1)} %get-tuple-element.7, f32[768]{0:T(1024)S(1)} %get-tuple-element.6), channel_id=1, replica_groups=mesh['row'=4,'col'=8] {'col'}, use_global_device_ids=true, to_apply=%region_3.0 | all-reduce | flops 1536 | bytes 12288 | tf_op jit(solution)/shard_map/psum | solution.py:47
  27.8 1.7 add_convert_fusion
  29.5 1.6 collective-permute-start.1
  31.1 1.5 collective-permute-start
  32.6 47.3 %collective-permute-done.1 = bf16[768,1536]{1,0:T(8,128)(2,1)S(1)} collective-permute-done((bf16[768,1536]{1,0:T(8,128)(2,1)}, bf16[768,1536]{1,0:T(8,128)(2,1)S(1)}, u32[]{:S(2)}, u32[]{:S(2)}) %collective-permute-start.1) | collective-permute-done | bytes 2359328 | tf_op jit(solution)/shard_map/ppermute | solution.py:18
  80.0 1.2 slice.40
  81.1 1.5 collective-permute-start.2
  82.6 1.1 slice.41
  83.7 1.5 collective-permute-start.3
  85.2 21.2 %collective-permute-done.2 = bf16[384,1536]{1,0:T(8,128)(2,1)S(1)} collective-permute-done((bf16[384,1536]{1,0:T(8,128)(2,1)}, bf16[384,1536]{1,0:T(8,128)(2,1)S(1)}, u32[]{:S(2)}, u32[]{:S(2)}) %collective-permute-start.2) | collective-permute-done | bytes 1179680 | tf_op jit(solution)/shard_map/ppermute | solution.py:18
  106.5 1.5 fusion.143
  108.0 2.6 fusion.131
  110.6 1.8 convolution_add_fusion.1
  112.4 2.1 fusion.141
  114.6 3.3 fusion.35
  117.9 1.5 fusion.147
  119.5 2.0 fusion.145
  121.5 2.6 fusion.135
  124.1 1.9 convolution_add_fusion.3
  126.0 3.2 fusion.27
  129.3 0.2 all-gather.7.cloned.1.call-start
  129.5 1.6 fusion.151
  131.1 2.0 fusion.149
  133.1 2.6 fusion.139
  135.7 1.9 convolution_add_fusion.5
  137.7 3.4 fusion.19
  141.1 0.5 collective-permute-start.5
  141.7 1.5 collective-permute-start.4
  143.1 47.8 %collective-permute-done.5 = bf16[384,3072]{1,0:T(8,128)(2,1)S(1)} collective-permute-done((bf16[384,3072]{1,0:T(8,128)(2,1)S(1)}, bf16[384,3072]{1,0:T(8,128)(2,1)S(1)}, u32[]{:S(2)}, u32[]{:S(2)}) %collective-permute-start.5) | collective-permute-done | bytes 2359328 | tf_op jit(solution)/shard_map/ppermute | solution.py:18
  191.0 1.5 copy-done.15
  192.4 1.1 slice.42
  193.5 1.5 collective-permute-start.6
  195.0 2.3 fusion.185
  197.3 1.9 copy.20
  199.2 1.9 copy.22
  201.2 1.9 copy.24
  203.1 2.3 fusion.184
  205.4 1.9 copy.19
  207.3 2.0 copy.23
  209.3 1.9 copy.21
  211.2 2.4 slice.43
  213.6 0.5 collective-permute-start.7
  214.0 3.3 collective-permute-done.6
  217.4 2.5 fusion.119
  219.8 30.3 %all-gather.9.cloned.1.call-done = bf16[12288,256]{0,1:T(8,128)(2,1)} async-done(((bf16[1536,256]{0,1:T(8,128)(2,1)}), bf16[12288,256]{0,1:T(8,128)(2,1)}) %all-gather.9.cloned.1.call-update) | async-done | bytes 6291472 | tf_op jit(solution)/shard_map/all_gather | solution.py:71
  250.2 2.7 fusion.123
  252.8 3.2 fusion.36
  256.0 3.3 fusion.42
  259.3 55.7 %all-gather.7.cloned.1.call-done = bf16[12288,256]{0,1:T(8,128)(2,1)} async-done(((bf16[1536,256]{0,1:T(8,128)(2,1)}), bf16[12288,256]{0,1:T(8,128)(2,1)}) %all-gather.7.cloned.1.call-update) | async-done | bytes 6291472 | tf_op jit(solution)/shard_map/all_gather | solution.py:71
  315.1 1.9 fusion.127
  316.9 3.3 fusion.48
  320.2 3.3 fusion.38
  323.5 2.7 fusion.44
  326.2 2.7 fusion.50
  328.9 2.1 fusion.117
  331.0 1.9 fusion.121
  332.9 2.0 fusion.125
  335.0 2.9 multiply_add_fusion
  337.9 1.1 multiply_add_fusion.1
  339.0 1.1 multiply_add_fusion.2
  340.3 1.4 copy.17
  341.7 1.4 copy.18
  (63 shorter events, 0.5 us)
Async XLA Ops:
  7.2 20.6 %copy-start.5 = (f32[384,768]{1,0:T(8,128)S(1)}, f32[384,768]{1,0:T(8,128)}, u32[]{:S(2)}) copy-start(f32[384,768]{1,0:T(8,128)} %param.9) | copy-start | bytes 3538948
  7.2 99.3 %all-gather.5.cloned.1.call-start = ((), (), s32[]{:S(2)}) async-start(), calls=%async_computation | async-start | bytes 5308416 | tf_op jit(solution)/shard_map/all_gather | solution.py:54
  29.5 187.9 %all-gather.11.cloned.1.call-start = ((), (), s32[]{:S(2)}) async-start(), calls=%async_computation.3 | async-start | bytes 7077888 | tf_op jit(solution)/shard_map/all_gather | solution.py:71
  29.5 50.4 %collective-permute-start.1 = (bf16[768,1536]{1,0:T(8,128)(2,1)}, bf16[768,1536]{1,0:T(8,128)(2,1)S(1)}, u32[]{:S(2)}, u32[]{:S(2)}) collective-permute-start(bf16[768,1536]{1,0:T(8,128)(2,1)} %param.14), channel_id=1, source_target_pairs={{0,16},{8,24},{16,0},{24,8},{1,17},{9,25},{17,1},{25,9},{2,18},{10... | collective-permute-start | bytes 7077896 | tf_op jit(solution)/shard_map/ppermute | solution.py:18
  31.1 51.5 %collective-permute-start = (bf16[768,1536]{1,0:T(8,128)(2,1)}, bf16[768,1536]{1,0:T(8,128)(2,1)S(1)}, u32[]{:S(2)}, u32[]{:S(2)}) collective-permute-start(bf16[768,1536]{1,0:T(8,128)(2,1)} %param.14), channel_id=1, source_target_pairs={{0,8},{8,0},{16,24},{24,16},{1,9},{9,1},{17,25},{25,17},{2,10},{10... | collective-permute-start | bytes 7077896 | tf_op jit(solution)/shard_map/ppermute | solution.py:18
  79.9 3.8 %copy-start = (bf16[768,1536]{1,0:T(8,128)(2,1)}, bf16[768,1536]{1,0:T(8,128)(2,1)S(1)}, u32[]{:S(2)}) copy-start(bf16[768,1536]{1,0:T(8,128)(2,1)S(1)} %collective-permute-done.1) | copy-start | bytes 7077892
  81.1 25.3 %collective-permute-start.2 = (bf16[384,1536]{1,0:T(8,128)(2,1)}, bf16[384,1536]{1,0:T(8,128)(2,1)S(1)}, u32[]{:S(2)}, u32[]{:S(2)}) collective-permute-start(bf16[384,1536]{1,0:T(8,128)(2,1)} %slice.40), channel_id=1, source_target_pairs={{0,8},{8,0},{16,24},{24,16},{1,9},{9,1},{17,25},{25,17},{2,10},{10... | collective-permute-start | bytes 3538952 | tf_op jit(solution)/shard_map/ppermute | solution.py:18
  83.7 28.7 %collective-permute-start.3 = (bf16[384,1536]{1,0:T(8,128)(2,1)}, bf16[384,1536]{1,0:T(8,128)(2,1)}, u32[]{:S(2)}, u32[]{:S(2)}) collective-permute-start(bf16[384,1536]{1,0:T(8,128)(2,1)} %slice.41), channel_id=1, source_target_pairs={{0,16},{8,24},{16,0},{24,8},{1,17},{9,25},{17,1},{25,9},{2,18},{10... | collective-permute-start | bytes 3538952 | tf_op jit(solution)/shard_map/ppermute | solution.py:18
  112.4 2.2 copy-start.1
  112.4 2.2 copy-start.19
  117.9 132.3 %all-gather.9.cloned.1.call-start = ((), (), s32[]{:S(2)}) async-start(), calls=%async_computation.2 | async-start | bytes 7077888 | tf_op jit(solution)/shard_map/all_gather | solution.py:71
  124.1 2.0 copy-start.2
  129.3 185.7 %all-gather.7.cloned.1.call-start = ((), (), s32[]{:S(2)}) async-start(), calls=%async_computation.1 | async-start | bytes 7077888 | tf_op jit(solution)/shard_map/all_gather | solution.py:71
  135.7 2.0 copy-start.3
  137.7 3.4 copy-start.4
  141.1 49.8 %collective-permute-start.5 = (bf16[384,3072]{1,0:T(8,128)(2,1)S(1)}, bf16[384,3072]{1,0:T(8,128)(2,1)S(1)}, u32[]{:S(2)}, u32[]{:S(2)}) collective-permute-start(bf16[384,3072]{1,0:T(8,128)(2,1)S(1)} %copy-done.4), channel_id=1, source_target_pairs={{0,16},{8,24},{16,0},{24,8},{1,17},{9,25},{17,1},{25,9},{2,18},{10... | collective-permute-start | bytes 7077896 | tf_op jit(solution)/shard_map/ppermute | solution.py:18
  141.7 69.6 %collective-permute-start.4 = (bf16[384,3072]{1,0:T(8,128)(2,1)S(1)}, bf16[384,3072]{1,0:T(8,128)(2,1)}, u32[]{:S(2)}, u32[]{:S(2)}) collective-permute-start(bf16[384,3072]{1,0:T(8,128)(2,1)S(1)} %copy-done.4), channel_id=1, source_target_pairs={{0,8},{8,0},{16,24},{24,16},{1,9},{9,1},{17,25},{25,17},{2,10},{10... | collective-permute-start | bytes 7077896 | tf_op jit(solution)/shard_map/ppermute | solution.py:18
  190.9 1.5 copy-start.15
  193.5 23.9 %collective-permute-start.6 = (bf16[384,1536]{1,0:T(8,128)(2,1)}, bf16[384,1536]{1,0:T(8,128)(2,1)S(1)}, u32[]{:S(2)}, u32[]{:S(2)}) collective-permute-start(bf16[384,1536]{1,0:T(8,128)(2,1)} %slice.42), channel_id=1, source_target_pairs={{0,8},{8,0},{16,24},{24,16},{1,9},{9,1},{17,25},{25,17},{2,10},{10... | collective-permute-start | bytes 3538952 | tf_op jit(solution)/shard_map/ppermute | solution.py:18
  213.6 115.3 %collective-permute-start.7 = (bf16[384,1536]{1,0:T(8,128)(2,1)}, bf16[384,1536]{1,0:T(8,128)(2,1)}, u32[]{:S(2)}, u32[]{:S(2)}) collective-permute-start(bf16[384,1536]{1,0:T(8,128)(2,1)} %slice.43), channel_id=1, source_target_pairs={{0,16},{8,24},{16,0},{24,8},{1,17},{9,25},{17,1},{25,9},{2,18},{10... | collective-permute-start | bytes 3538952 | tf_op jit(solution)/shard_map/ppermute | solution.py:18
  250.1 2.7 copy-start.16
  315.1 8.4 %slice-start = ((s8[6291456]{0:T(1024)(128)(4,1)}), s8[4194304]{0:T(1024)(128)(4,1)S(1)}, s32[]{:S(2)}) async-start(s8[6291456]{0:T(1024)(128)(4,1)} %bitcast.48), calls=%async_computation.4 | async-start | bytes 8388608
  316.9 6.6 %slice-start.1 = ((s8[6291456]{0:T(1024)(128)(4,1)}), s8[2097152]{0:T(1024)(128)(4,1)S(1)}, s32[]{:S(2)}) async-start(s8[6291456]{0:T(1024)(128)(4,1)} %bitcast.48), calls=%async_computation.5 | async-start | bytes 4194304
  320.2 6.0 %copy-start.6 = (bf16[12288,256]{0,1:T(8,128)(2,1)S(1)}, bf16[12288,256]{0,1:T(8,128)(2,1)}, u32[]{:S(2)}) copy-start(bf16[12288,256]{0,1:T(8,128)(2,1)} %all-gather.7.cloned.1.call-done) | copy-start | bytes 18874372
  332.8 2.0 copy-start.8
  332.8 2.0 copy-start.12
  332.8 2.0 copy-start.14
  332.9 2.0 copy-start.18
  332.9 2.0 copy-start.20
  332.9 2.0 copy-start.21
  334.9 2.9 copy-start.7
  334.9 2.9 copy-start.11
  334.9 2.9 copy-start.13
  335.0 2.9 copy-start.17
  337.9 1.1 copy-start.9
  337.9 1.1 copy-start.10
Sparse Core Ops, SparseCore 0:
  29.6 49.9 all-gather.4
  118.0 67.0 all-gather.10
  186.7 63.3 all-gather.8
  251.6 63.3 all-gather.6

commit v2 on v0

--- a/solution.py
+++ b/solution.py
@@ -13,23 +13,98 @@
 sigma_now = 0.322
 
 
+def flipped(value, axis, bits):
+    devices = lax.axis_size(axis)
+    return lax.ppermute(value, axis, [(i, i ^ bits) for i in range(devices)])
+
+
+def spread_blocks(block, dim, axis):
+    half = block.shape[dim] // 2
+    held = {0: block}
+    pieces = {0: [(0, block)]}
+    order = sorted(range(1, lax.axis_size(axis)), key=lambda k: (k.bit_count(), k))
+    for k in order:
+        low = k & -k
+        high = 1 << (k.bit_length() - 1)
+        if low == high:
+            held[k] = flipped(block, axis, k)
+            pieces[k] = [(0, held[k])]
+        else:
+            first = lax.slice_in_dim(held[k ^ low], 0, half, axis=dim)
+            second = lax.slice_in_dim(held[k ^ high], half, 2 * half, axis=dim)
+            first, second = flipped(first, axis, low), flipped(second, axis, high)
+            pieces[k] = [(0, first), (half, second)]
+            if k.bit_count() < lax.axis_size(axis).bit_length() - 1:
+                held[k] = lax.concatenate([first, second], dim)
+    return pieces, held
+
+
+def chain_step(value, moves):
+    return lax.ppermute(
+        value, "col", [(2 * a + core, 2 * b + core) for a, b in moves for core in range(2)]
+    )
+
+
+def gather_chain(hidden):
+    chips = lax.axis_size("col") // 2
+    chip = lax.axis_index("col") // 2
+    blocks = [(chip, hidden)]
+    upward = downward = hidden
+    for step in range(1, chips):
+        up = [(a, a + 1) for a in range(step - 1, chips - 1)]
+        down = [(a, a - 1) for a in range(1, chips - step + 1)]
+        if 2 * step > chips + 1:
+            upward = downward = chain_step(upward, up + down)
+        else:
+            upward, downward = chain_step(upward, up), chain_step(downward, down)
+            if 2 * step > chips - 1:
+                upward = downward = jnp.where(chip >= step, upward, downward)
+        if 2 * step > chips - 1:
+            blocks.append((jnp.where(chip >= step, chip - step, jnp.minimum(chip + step, chips - 1)), upward))
+        else:
+            blocks.append((jnp.maximum(chip - step, 0), upward))
+            blocks.append((jnp.minimum(chip + step, chips - 1), downward))
+    return blocks
+
+
 def on_device(state, noise, mod_shift, mod_scale, mod_gate, w_in, b_in, w_out, b_out):
-    w_in_all = lax.all_gather(w_in, "row", axis=0, tiled=True)
-    w_out_all = lax.all_gather(w_out, "row", axis=1, tiled=True)
-    col_sums, squares = lax.psum((jnp.sum(state, axis=0), jnp.sum(state * state, axis=0)), "col")
-    center = col_sums / D
-    spread = squares / D - center * center
+    row = lax.axis_index("row")
+    core = lax.axis_index("col") % 2
+    in_pieces, _ = spread_blocks(w_in, 0, "row")
+    sums = jnp.stack((jnp.sum(state, axis=0), jnp.sum(state * state, axis=0)))
+    bits = 1
+    while bits < lax.axis_size("col"):
+        sums = sums + flipped(sums, "col", bits)
+        bits *= 2
+    center = sums[0] / D
+    spread = sums[1] / D - center * center
     normed = (
         (state - center[None, :]) * lax.rsqrt(spread[None, :] + 1e-06) * (1.0 + mod_scale[:, None])
         + mod_shift[:, None]
     ).astype(jnp.bfloat16)
     normed_all = lax.all_gather(normed, "col", axis=0, tiled=True)
-    pre_act = lax.dot_general(
-        w_in_all, normed_all, (((0,), (0,)), ((), ())), preferred_element_type=jnp.float32
-    )
+
+    pre_act = None
+    for k, parts in in_pieces.items():
+        for offset, piece in parts:
+            start = (row ^ k) * w_in.shape[0] + offset
+            part = lax.dynamic_slice_in_dim(normed_all, start, piece.shape[0], axis=0)
+            term = lax.dot_general(
+                piece, part, (((0,), (0,)), ((), ())), preferred_element_type=jnp.float32
+            )
+            pre_act = term if pre_act is None else pre_act + term
     hidden = jax.nn.gelu(pre_act + b_in[:, None], approximate=True).astype(jnp.bfloat16)
-    hidden_all = lax.all_gather(hidden, "col", axis=0, tiled=True)
-    mixed_out = jnp.dot(w_out_all, hidden_all, preferred_element_type=jnp.float32)
+    last = list(in_pieces.values())[-1]
+    w_out, *_ = lax.optimization_barrier((w_out, *[piece for _, piece in last]))
+    w_out_all = lax.all_gather(w_out, "row", axis=1, tiled=True)
+
+    mixed_out = None
+    units = w_in.shape[1]
+    for owner, block in gather_chain(hidden):
+        for near, value in ((core, block), (1 - core, flipped(block, "col", 1))):
+            weights = lax.dynamic_slice_in_dim(w_out_all, (2 * owner + near) * units, units, axis=1)
+            term = jnp.dot(weights, value, preferred_element_type=jnp.float32)
+            mixed_out = term if mixed_out is None else mixed_out + term
     branch = mixed_out + b_out[:, None]
     predicted = state + mod_gate[:, None] * branch
     purified = (

time: 474 us -> 314 us (0.66)
  waiting for transfers between devices: 399 us -> 224 us
  starting transfers between devices: 0.16 us -> 24.4 us
  blocking collectives: 18.3 us -> 0 us
  matrix products: 31.4 us -> 42.4 us
  local copies, waits for them, and re-layouts: 6.13 us -> 0.8 us
    all_gather x2 -> x0, waiting for transfers between devices: 267 us -> none  [the longest x1 170 us: on_device(): hidden_all = lax.all_gather(hidden, 'col', axis=0, tiled=True)]
    ppermute x0 -> x17, waiting for transfers between devices: none -> 224 us  [the longest x5 148 us: chain_step(): lax.ppermute(value, 'col', [(2 * a + core, 2 * b + core) for a, b in move...]
    all_gather x1, waiting for transfers between devices: 82.4 us -> 0.01 us  [on_device(): w_out_all = lax.all_gather(w_out, 'row', axis=1, tiled=True)]
    all_gather x1, waiting for transfers between devices: 48.5 us -> 0.02 us  [on_device(): normed_all = lax.all_gather(normed, 'col', axis=0, tiled=True)]
    ppermute x0 -> x17, starting transfers between devices: none -> 24.3 us  [the longest x12 13.5 us: flipped(): return lax.ppermute(value, axis, [(i, i ^ bits) for i in range(devices)])]
    psum x1 -> x0, blocking collectives: 18.3 us -> none  [on_device(): lax.psum((jnp.sum(state, axis=0), jnp.sum(state * state, axis=0)), 'col')]
    dot_general x2 -> x15, matrix products: 31.4 us -> 42.4 us  [the longest x10 30.4 us: on_device(): term = jnp.dot(weights, value, preferred_element_type=jnp.float32)]
    unnamed x14 -> x24, local copies, waits for them, and re-layouts: 6.13 us -> 0.63 us
  transfers between devices with their start and end apart: 4 -> 19, of which waited for: 4 -> 11; matrix products, arithmetic and copies ran while one was open for 3% -> 13% of each run, Pallas kernels for 0% -> 0%
where the time goes in v2:
time: 314 us
  waiting for transfers between devices  224 us (71%)
  matrix products  42.4 us (14%)
  starting transfers between devices  24.4 us (8%)
  between operations  14.4 us (5%)
  other arithmetic  7.78 us (2%)
    ppermute x5, waiting for transfers between devices, chain_step(): lax.ppermute(value, 'col', [(2 * a + core, 2 * b + core) for a, b in move...  148 us
    ppermute x12, waiting for transfers between devices, flipped(): return lax.ppermute(value, axis, [(i, i ^ bits) for i in range(devices)])  75.7 us
    dot_general x10, matrix products, on_device(): term = jnp.dot(weights, value, preferred_element_type=jnp.float32)  30.4 us
    ppermute x12, starting transfers between devices, flipped(): return lax.ppermute(value, axis, [(i, i ^ bits) for i in range(devices)])  13.5 us
    dot_general x5, matrix products, on_device(): lax.dot_general(piece, part, (((0,), (0,)), ((), ())), preferred_element_...  12 us
    ppermute x5, starting transfers between devices, chain_step(): lax.ppermute(value, 'col', [(2 * a + core, 2 * b + core) for a, b in move...  10.8 us
  transfers between devices with their start and end apart: 19, of which 11 were waited for; matrix products, arithmetic and copies ran while one was open for 13% of the time, Pallas kernels for 0%

profile of v2, /device:TPU:0, one launch (start us, length us, event | category | flops | bytes accessed | tf_op | source)
XLA Modules:
  0.0 313.5 jit_solution(14306768916896562773)
XLA Ops:
  7.2 0.0 all-gather.5.cloned.1.call-start
  7.2 1.4 fusion.60
  8.7 0.5 collective-permute-start.4
  9.2 0.8 collective-permute-done.4
  10.0 3.0 collective-permute-start.5
  13.0 1.6 collective-permute-done.5
  14.6 3.1 collective-permute-start.6
  17.7 0.7 broadcast_add_fusion
  18.4 0.9 collective-permute-done.6
  19.4 2.3 add_convert_fusion
  21.7 0.0 all-gather.5.cloned.1.call-update
  21.7 0.0 all-gather.3.cloned.1.call-start
  21.7 1.9 collective-permute-start
  23.7 1.5 collective-permute-start.2
  25.1 48.2 %collective-permute-done = bf16[768,1536]{1,0:T(8,128)(2,1)S(1)} collective-permute-done((bf16[768,1536]{1,0:T(8,128)(2,1)}, bf16[768,1536]{1,0:T(8,128)(2,1)S(1)}, u32[]{:S(2)}, u32[]{:S(2)}) %collective-permute-start) | collective-permute-done | bytes 2359328 | tf_op jit(solution)/shard_map/ppermute | solution.py:18
  73.3 0.1 slice.16
  73.4 1.6 collective-permute-start.1
  75.0 0.7 collective-permute-done.2
  75.8 0.1 slice.17
  75.8 0.8 collective-permute-start.3
  76.7 23.2 %collective-permute-done.1 = bf16[384,1536]{1,0:T(8,128)(2,1)S(1)} collective-permute-done((bf16[384,1536]{1,0:T(8,128)(2,1)S(1)}, bf16[384,1536]{1,0:T(8,128)(2,1)S(1)}, u32[]{:S(2)}, u32[]{:S(2)}) %collective-permute-start.1) | collective-permute-done | bytes 1179680 | tf_op jit(solution)/shard_map/ppermute | solution.py:18
  99.9 0.2 collective-permute-done.3
  100.1 0.0 all-gather.3.cloned.1.call-update
  100.1 0.0 all-gather.5.cloned.1.call-done
  100.2 2.6 fusion.40
  102.8 0.6 copy-done.7
  103.4 2.0 fusion.28
  105.4 0.0 copy-start.11
  105.5 2.0 fusion.30
  107.5 0.0 copy-start.8
  107.5 2.0 fusion.32
  109.6 3.3 %fusion.7 = bf16[1536,768]{0,1:T(8,128)(2,1)S(1)} fusion(f32[768,1536]{1,0:T(8,128)S(1)} %fusion.40, f32[768,1536]{1,0:T(8,128)S(1)} %fusion.28, f32[768,1536]{1,0:T(8,128)S(1)} %fusion.32, f32[768,1536]{1,0:T(8,128)S(1)} %fusion.30, f32[1536]{0:T(1024)S(1)} %copy-done.8, bf16[384,1536]{1,0:T(8,128)(2,1)S(1)} %collective-permute-done.3, ...), kind=kOutput, calls=%fused_computation.8 | convolution fusion | flops 922484736 | bytes 23011332 | tf_op jit(solution)/shard_map/dot_general | solution.py:92
  112.9 4.7 %collective-permute-start.8 = (bf16[1536,768]{0,1:T(8,128)(2,1)S(1)}, bf16[1536,768]{0,1:T(8,128)(2,1)}, u32[]{:S(2)}, u32[]{:S(2)}) collective-permute-start(bf16[1536,768]{0,1:T(8,128)(2,1)S(1)} %fusion.7), channel_id=1, source_target_pairs={{0,2},{1,3},{2,4},{3,5},{4,6},{5,7},{8,10},{9,11},{10,12},{11,13},... | collective-permute-start | bytes 7077896 | tf_op jit(solution)/shard_map/ppermute | solution.py:43
  117.6 1.3 collective-permute-start.10
  118.9 45.5 %collective-permute-done.8 = bf16[1536,768]{0,1:T(8,128)(2,1)} collective-permute-done((bf16[1536,768]{0,1:T(8,128)(2,1)S(1)}, bf16[1536,768]{0,1:T(8,128)(2,1)}, u32[]{:S(2)}, u32[]{:S(2)}) %collective-permute-start.8) | collective-permute-done | bytes 2359328 | tf_op jit(solution)/shard_map/ppermute | solution.py:43
  164.4 2.0 collective-permute-start.12
  166.5 3.6 %collective-permute-done.10 = bf16[1536,768]{0,1:T(8,128)(2,1)} collective-permute-done((bf16[1536,768]{0,1:T(8,128)(2,1)S(1)}, bf16[1536,768]{0,1:T(8,128)(2,1)}, u32[]{:S(2)}, u32[]{:S(2)}) %collective-permute-start.10) | collective-permute-done | bytes 2359328 | tf_op jit(solution)/shard_map/ppermute | solution.py:43
  170.1 1.3 collective-permute-start.13
  171.4 0.0 collective-permute-done.12
  171.4 50.5 %collective-permute-done.13 = bf16[1536,768]{0,1:T(8,128)(2,1)} collective-permute-done((bf16[1536,768]{0,1:T(8,128)(2,1)}, bf16[1536,768]{0,1:T(8,128)(2,1)}, u32[]{:S(2)}, u32[]{:S(2)}) %collective-permute-start.13) | collective-permute-done | bytes 2359328 | tf_op jit(solution)/shard_map/ppermute | solution.py:43
  221.9 3.3 %broadcast_select_fusion = bf16[1536,768]{0,1:T(8,128)(2,1)} fusion(bf16[1536,768]{0,1:T(8,128)(2,1)} %collective-permute-done.12, bf16[1536,768]{0,1:T(8,128)(2,1)} %collective-permute-done.13, pred[]{:T(512)S(6)} %ge.7), kind=kLoop, calls=%fused_computation.9 | loop fusion | flops 1179648 | bytes 7077889 | tf_op jit(solution)/shard_map/jit(_where)/select_n | solution.py:61
  225.2 1.5 collective-permute-start.15
  226.7 0.1 collective-permute-start.14
  226.7 0.5 collective-permute-start.7
  227.2 0.1 collective-permute-start.9
  227.3 0.4 collective-permute-start.11
  227.7 48.3 %collective-permute-done.15 = bf16[1536,768]{0,1:T(8,128)(2,1)} collective-permute-done((bf16[1536,768]{0,1:T(8,128)(2,1)}, bf16[1536,768]{0,1:T(8,128)(2,1)}, u32[]{:S(2)}, u32[]{:S(2)}) %collective-permute-start.15) | collective-permute-done | bytes 2359328 | tf_op jit(solution)/shard_map/ppermute | solution.py:43
  276.1 0.0 collective-permute-start.16
  276.1 2.5 fusion.34
  278.6 3.6 %fusion.23 = f32[384,768]{1,0:T(8,128)S(1)} fusion(bf16[1536,768]{0,1:T(8,128)(2,1)} %collective-permute-done.10, bf16[384,12288]{1,0:T(8,128)(2,1)} %all-gather.3.cloned.1.call-done, s32[]{:T(128)S(6)} %select_n.81), kind=kOutput, calls=%fused_computation.31 | convolution fusion | flops 905969664 | bytes 4718596 | tf_op jit(solution)/shard_map/dot_general | solution.py:106
  282.2 2.8 fusion.20
  285.0 2.8 fusion.16
  287.8 0.0 collective-permute-done.14
  287.8 2.8 fusion.18
  290.6 0.0 collective-permute-done.7
  290.6 2.8 convolution_add_fusion.4
  293.4 2.8 convolution_add_fusion.3
  296.2 2.8 fusion.14
  299.0 0.0 copy-start
  299.1 0.0 copy-start.1
  299.1 0.0 copy-start.9
  299.1 0.0 copy-start.10
  299.1 3.1 fusion.13
  302.2 4.5 %multiply_add_fusion = (f32[384,768]{1,0:T(8,128)}, f32[384,768]{1,0:T(8,128)}) fusion(f32[384,768]{1,0:T(8,128)S(1)} %copy-done.1, f32[384,768]{1,0:T(8,128)S(1)} %copy-done, f32[384]{0:T(512)S(1)} %copy-done.9, f32[384,768]{1,0:T(8,128)S(1)} %fusion.13, bf16[1536,768]{0,1:T(8,128)(2,1)} %collective-permute-done.16, bf16[384,12288]{1,0:T(8,128)(2,1)S(1)} %copy-done.2, ...), kind=kOutput, calls=%fused_computation.22 | convolution fusion | flops 908623872 | bytes 9441284 | tf_op jit(solution)/shard_map/dot_general | solution.py:106
  (28 shorter events, 0.1 us)
Async XLA Ops:
  7.2 93.0 %all-gather.5.cloned.1.call-start = ((), (), s32[]{:S(2)}) async-start(), calls=%async_computation.1 | async-start | bytes 5308416 | tf_op jit(solution)/shard_map/all_gather | solution.py:85
  8.7 1.3 collective-permute-start.4
  10.0 4.6 %collective-permute-start.5 = (f32[2,768]{1,0:T(2,128)S(1)}, f32[2,768]{1,0:T(2,128)S(1)}, u32[]{:S(2)}, u32[]{:S(2)}) collective-permute-start(f32[2,768]{1,0:T(2,128)S(1)} %fusion.59), channel_id=1, source_target_pairs={{0,2},{1,3},{2,0},{3,1},{4,6},{5,7},{6,4},{7,5},{8,10},{9,11},{10,... | collective-permute-start | bytes 18440 | tf_op jit(solution)/shard_map/ppermute | solution.py:18
  14.6 4.7 %collective-permute-start.6 = (f32[2,768]{1,0:T(2,128)S(1)}, f32[2,768]{1,0:T(2,128)S(1)}, u32[]{:S(2)}, u32[]{:S(2)}) collective-permute-start(f32[2,768]{1,0:T(2,128)S(1)} %fusion.76), channel_id=1, source_target_pairs={{0,4},{1,5},{2,6},{3,7},{4,0},{5,1},{6,2},{7,3},{8,12},{9,13},{10,... | collective-permute-start | bytes 18440 | tf_op jit(solution)/shard_map/ppermute | solution.py:18
  21.7 254.4 %all-gather.3.cloned.1.call-start = ((), (), s32[]{:S(2)}) async-start(), calls=%async_computation | async-start | bytes 11796480 | tf_op jit(solution)/shard_map/all_gather | solution.py:99
  21.7 51.6 %collective-permute-start = (bf16[768,1536]{1,0:T(8,128)(2,1)}, bf16[768,1536]{1,0:T(8,128)(2,1)S(1)}, u32[]{:S(2)}, u32[]{:S(2)}) collective-permute-start(bf16[768,1536]{1,0:T(8,128)(2,1)} %param.14), channel_id=1, source_target_pairs={{0,16},{8,24},{16,0},{24,8},{1,17},{9,25},{17,1},{25,9},{2,18},{10... | collective-permute-start | bytes 7077896 | tf_op jit(solution)/shard_map/ppermute | solution.py:18
  23.7 52.1 %collective-permute-start.2 = (bf16[768,1536]{1,0:T(8,128)(2,1)}, bf16[768,1536]{1,0:T(8,128)(2,1)S(1)}, u32[]{:S(2)}, u32[]{:S(2)}) collective-permute-start(bf16[768,1536]{1,0:T(8,128)(2,1)} %param.14), channel_id=1, source_target_pairs={{0,8},{8,0},{16,24},{24,16},{1,9},{9,1},{17,25},{25,17},{2,10},{10... | collective-permute-start | bytes 7077896 | tf_op jit(solution)/shard_map/ppermute | solution.py:18
  73.3 1.7 copy-start.3
  73.4 26.5 %collective-permute-start.1 = (bf16[384,1536]{1,0:T(8,128)(2,1)S(1)}, bf16[384,1536]{1,0:T(8,128)(2,1)S(1)}, u32[]{:S(2)}, u32[]{:S(2)}) collective-permute-start(bf16[384,1536]{1,0:T(8,128)(2,1)S(1)} %slice.16), channel_id=1, source_target_pairs={{0,8},{8,0},{16,24},{24,16},{1,9},{9,1},{17,25},{25,17},{2,10},{10... | collective-permute-start | bytes 3538952 | tf_op jit(solution)/shard_map/ppermute | solution.py:18
  75.8 24.1 %copy-start.5 = (bf16[768,1536]{1,0:T(8,128)(2,1)}, bf16[768,1536]{1,0:T(8,128)(2,1)S(1)}, u32[]{:S(2)}) copy-start(bf16[768,1536]{1,0:T(8,128)(2,1)S(1)} %collective-permute-done.2) | copy-start | bytes 7077892
  75.8 24.2 %collective-permute-start.3 = (bf16[384,1536]{1,0:T(8,128)(2,1)S(1)}, bf16[384,1536]{1,0:T(8,128)(2,1)S(1)}, u32[]{:S(2)}, u32[]{:S(2)}) collective-permute-start(bf16[384,1536]{1,0:T(8,128)(2,1)S(1)} %slice.17), channel_id=1, source_target_pairs={{0,16},{8,24},{16,0},{24,8},{1,17},{9,25},{17,1},{25,9},{2,18},{10... | collective-permute-start | bytes 3538952 | tf_op jit(solution)/shard_map/ppermute | solution.py:18
  100.2 2.7 copy-start.4
  100.2 3.2 %copy-start.7 = (bf16[3072,768]{1,0:T(8,128)(2,1)S(1)}, bf16[3072,768]{1,0:T(8,128)(2,1)}, u32[]{:S(2)}) copy-start(bf16[3072,768]{1,0:T(8,128)(2,1)} %all-gather.5.cloned.1.call-done) | copy-start | bytes 14155780
  103.4 2.0 copy-start.6
  105.4 2.1 copy-start.11
  107.5 2.1 copy-start.8
  112.9 51.5 %collective-permute-start.8 = (bf16[1536,768]{0,1:T(8,128)(2,1)S(1)}, bf16[1536,768]{0,1:T(8,128)(2,1)}, u32[]{:S(2)}, u32[]{:S(2)}) collective-permute-start(bf16[1536,768]{0,1:T(8,128)(2,1)S(1)} %fusion.7), channel_id=1, source_target_pairs={{0,2},{1,3},{2,4},{3,5},{4,6},{5,7},{8,10},{9,11},{10,12},{11,13},... | collective-permute-start | bytes 7077896 | tf_op jit(solution)/shard_map/ppermute | solution.py:43
  117.6 52.4 %collective-permute-start.10 = (bf16[1536,768]{0,1:T(8,128)(2,1)S(1)}, bf16[1536,768]{0,1:T(8,128)(2,1)}, u32[]{:S(2)}, u32[]{:S(2)}) collective-permute-start(bf16[1536,768]{0,1:T(8,128)(2,1)S(1)} %fusion.7), channel_id=1, source_target_pairs={{2,0},{3,1},{4,2},{5,3},{6,4},{7,5},{10,8},{11,9},{12,10},{13,11},... | collective-permute-start | bytes 7077896 | tf_op jit(solution)/shard_map/ppermute | solution.py:43
  164.4 7.0 %collective-permute-start.12 = (bf16[1536,768]{0,1:T(8,128)(2,1)}, bf16[1536,768]{0,1:T(8,128)(2,1)}, u32[]{:S(2)}, u32[]{:S(2)}) collective-permute-start(bf16[1536,768]{0,1:T(8,128)(2,1)} %collective-permute-done.8), channel_id=1, source_target_pairs={{2,4},{3,5},{4,6},{5,7},{10,12},{11,13},{12,14},{13,15},{18,20},{1... | collective-permute-start | bytes 7077896 | tf_op jit(solution)/shard_map/ppermute | solution.py:43
  170.1 51.8 %collective-permute-start.13 = (bf16[1536,768]{0,1:T(8,128)(2,1)}, bf16[1536,768]{0,1:T(8,128)(2,1)}, u32[]{:S(2)}, u32[]{:S(2)}) collective-permute-start(bf16[1536,768]{0,1:T(8,128)(2,1)} %collective-permute-done.10), channel_id=1, source_target_pairs={{2,0},{3,1},{4,2},{5,3},{10,8},{11,9},{12,10},{13,11},{18,16},{19,... | collective-permute-start | bytes 7077896 | tf_op jit(solution)/shard_map/ppermute | solution.py:43
  225.2 50.9 %collective-permute-start.15 = (bf16[1536,768]{0,1:T(8,128)(2,1)}, bf16[1536,768]{0,1:T(8,128)(2,1)}, u32[]{:S(2)}, u32[]{:S(2)}) collective-permute-start(bf16[1536,768]{0,1:T(8,128)(2,1)} %broadcast_select_fusion), channel_id=1, source_target_pairs={{4,6},{5,7},{2,0},{3,1},{12,14},{13,15},{10,8},{11,9},{20,22},{21,... | collective-permute-start | bytes 7077896 | tf_op jit(solution)/shard_map/ppermute | solution.py:43
  226.7 61.2 %collective-permute-start.14 = (bf16[1536,768]{0,1:T(8,128)(2,1)}, bf16[1536,768]{0,1:T(8,128)(2,1)}, u32[]{:S(2)}, u32[]{:S(2)}) collective-permute-start(bf16[1536,768]{0,1:T(8,128)(2,1)} %broadcast_select_fusion), channel_id=1, source_target_pairs={{0,1},{1,0},{2,3},{3,2},{4,5},{5,4},{6,7},{7,6},{8,9},{9,8},{10,11... | collective-permute-start | bytes 7077896 | tf_op jit(solution)/shard_map/ppermute | solution.py:18
  226.7 63.9 %collective-permute-start.7 = (bf16[1536,768]{0,1:T(8,128)(2,1)S(1)}, bf16[1536,768]{0,1:T(8,128)(2,1)}, u32[]{:S(2)}, u32[]{:S(2)}) collective-permute-start(bf16[1536,768]{0,1:T(8,128)(2,1)S(1)} %fusion.7), channel_id=1, source_target_pairs={{0,1},{1,0},{2,3},{3,2},{4,5},{5,4},{6,7},{7,6},{8,9},{9,8},{10,11... | collective-permute-start | bytes 7077896 | tf_op jit(solution)/shard_map/ppermute | solution.py:18
  227.2 69.0 %collective-permute-start.9 = (bf16[1536,768]{0,1:T(8,128)(2,1)}, bf16[1536,768]{0,1:T(8,128)(2,1)}, u32[]{:S(2)}, u32[]{:S(2)}) collective-permute-start(bf16[1536,768]{0,1:T(8,128)(2,1)} %collective-permute-done.8), channel_id=1, source_target_pairs={{0,1},{1,0},{2,3},{3,2},{4,5},{5,4},{6,7},{7,6},{8,9},{9,8},{10,11... | collective-permute-start | bytes 7077896 | tf_op jit(solution)/shard_map/ppermute | solution.py:18
  227.3 71.8 %collective-permute-start.11 = (bf16[1536,768]{0,1:T(8,128)(2,1)}, bf16[1536,768]{0,1:T(8,128)(2,1)}, u32[]{:S(2)}, u32[]{:S(2)}) collective-permute-start(bf16[1536,768]{0,1:T(8,128)(2,1)} %collective-permute-done.10), channel_id=1, source_target_pairs={{0,1},{1,0},{2,3},{3,2},{4,5},{5,4},{6,7},{7,6},{8,9},{9,8},{10,11... | collective-permute-start | bytes 7077896 | tf_op jit(solution)/shard_map/ppermute | solution.py:18
  276.1 26.1 %collective-permute-start.16 = (bf16[1536,768]{0,1:T(8,128)(2,1)}, bf16[1536,768]{0,1:T(8,128)(2,1)}, u32[]{:S(2)}, u32[]{:S(2)}) collective-permute-start(bf16[1536,768]{0,1:T(8,128)(2,1)} %collective-permute-done.15), channel_id=1, source_target_pairs={{0,1},{1,0},{2,3},{3,2},{4,5},{5,4},{6,7},{7,6},{8,9},{9,8},{10,11... | collective-permute-start | bytes 7077896 | tf_op jit(solution)/shard_map/ppermute | solution.py:18
  276.1 6.2 %copy-start.2 = (bf16[384,12288]{1,0:T(8,128)(2,1)S(1)}, bf16[384,12288]{1,0:T(8,128)(2,1)}, u32[]{:S(2)}) copy-start(bf16[384,12288]{1,0:T(8,128)(2,1)} %all-gather.3.cloned.1.call-done) | copy-start | bytes 28311556
  299.0 3.1 %copy-start = (f32[384,768]{1,0:T(8,128)S(1)}, f32[384,768]{1,0:T(8,128)}, u32[]{:S(2)}) copy-start(f32[384,768]{1,0:T(8,128)} %param.9) | copy-start | bytes 3538948
  299.1 3.1 %copy-start.1 = (f32[384,768]{1,0:T(8,128)S(1)}, f32[384,768]{1,0:T(8,128)}, u32[]{:S(2)}) copy-start(f32[384,768]{1,0:T(8,128)} %param.10) | copy-start | bytes 3538948
  299.1 3.1 %copy-start.9 = (f32[384]{0:T(512)S(1)}, f32[384]{0:T(512)}, u32[]{:S(2)}) copy-start(f32[384]{0:T(512)} %param.17) | copy-start | bytes 4612
  299.1 3.1 %copy-start.10 = (f32[384]{0:T(512)S(1)}, f32[384]{0:T(512)}, u32[]{:S(2)}) copy-start(f32[384]{0:T(512)} %param.13) | copy-start | bytes 4612
Sparse Core Ops, SparseCore 0:
  21.8 53.2 all-gather.4
  100.2 97.3 all-gather.2

commit v3 on v2

--- a/solution.py
+++ b/solution.py
@@ -48,22 +48,29 @@
 def gather_chain(hidden):
     chips = lax.axis_size("col") // 2
     chip = lax.axis_index("col") // 2
-    blocks = [(chip, hidden)]
+    blocks = [(chip, hidden, flipped(hidden, "col", 1))]
     upward = downward = hidden
     for step in range(1, chips):
         up = [(a, a + 1) for a in range(step - 1, chips - 1)]
         down = [(a, a - 1) for a in range(1, chips - step + 1)]
         if 2 * step > chips + 1:
+            owns, mains, others = zip(*blocks)
+            swapped = others[: -1]
+            upward, *swapped = lax.optimization_barrier((upward, *swapped))
+            blocks = list(zip(owns, mains, [*swapped, *others[-1:]]))
             upward = downward = chain_step(upward, up + down)
         else:
             upward, downward = chain_step(upward, up), chain_step(downward, down)
             if 2 * step > chips - 1:
                 upward = downward = jnp.where(chip >= step, upward, downward)
         if 2 * step > chips - 1:
-            blocks.append((jnp.where(chip >= step, chip - step, jnp.minimum(chip + step, chips - 1)), upward))
+            owner = jnp.where(chip >= step, chip - step, jnp.minimum(chip + step, chips - 1))
+            swapped = flipped(upward, "col", 1) if step < chips - 1 else None
+            blocks.append((owner, upward, swapped))
         else:
-            blocks.append((jnp.maximum(chip - step, 0), upward))
-            blocks.append((jnp.minimum(chip + step, chips - 1), downward))
+            for owner, block in ((chip - step, upward), (chip + step, downward)):
+                swapped = flipped(block, "col", 1) if step < chips - 1 else None
+                blocks.append((jnp.clip(owner, 0, chips - 1), block, swapped))
     return blocks
 
 
@@ -86,6 +93,9 @@
 
     pre_act = None
     for k, parts in in_pieces.items():
+        if k and len(parts) > 1:
+            pre_act, *arrived = lax.optimization_barrier((pre_act, *[piece for _, piece in parts]))
+            parts = [(offset, piece) for (offset, _), piece in zip(parts, arrived)]
         for offset, piece in parts:
             start = (row ^ k) * w_in.shape[0] + offset
             part = lax.dynamic_slice_in_dim(normed_all, start, piece.shape[0], axis=0)
@@ -94,14 +104,17 @@
             )
             pre_act = term if pre_act is None else pre_act + term
     hidden = jax.nn.gelu(pre_act + b_in[:, None], approximate=True).astype(jnp.bfloat16)
-    last = list(in_pieces.values())[-1]
-    w_out, *_ = lax.optimization_barrier((w_out, *[piece for _, piece in last]))
+    w_out, _ = lax.optimization_barrier((w_out, piece))
     w_out_all = lax.all_gather(w_out, "row", axis=1, tiled=True)
 
     mixed_out = None
     units = w_in.shape[1]
-    for owner, block in gather_chain(hidden):
-        for near, value in ((core, block), (1 - core, flipped(block, "col", 1))):
+    blocks = gather_chain(hidden)
+    for owner, block, swapped in blocks:
+        if swapped is None:
+            block, mixed_out = lax.optimization_barrier((block, mixed_out))
+            swapped = flipped(block, "col", 1)
+        for near, value in ((core, block), (1 - core, swapped)):
             weights = lax.dynamic_slice_in_dim(w_out_all, (2 * owner + near) * units, units, axis=1)
             term = jnp.dot(weights, value, preferred_element_type=jnp.float32)
             mixed_out = term if mixed_out is None else mixed_out + term

time: 314 us -> 290 us (0.924)
  waiting for transfers between devices: 224 us -> 188 us
  matrix products: 42.4 us -> 48.4 us
  local copies, waits for them, and re-layouts: 0.8 us -> 4.89 us
    ppermute x5, waiting for transfers between devices: 148 us -> 123 us  [chain_step(): lax.ppermute(value, 'col', [(2 * a + core, 2 * b + core) for a, b in move...]
    ppermute x12, waiting for transfers between devices: 75.7 us -> 65.7 us  [flipped(): return lax.ppermute(value, axis, [(i, i ^ bits) for i in range(devices)])]
    dot_general x5, matrix products: 12 us -> 19.1 us  [on_device(): lax.dot_general(piece, part, (((0,), (0,)), ((), ())), preferred_element_...]
  transfers between devices with their start and end apart: 19 -> 19, of which waited for: 11 -> 10; matrix products, arithmetic and copies ran while one was open for 13% -> 17% of each run, Pallas kernels for 0% -> 0%
where the time goes in v3:
time: 290 us; the launch traced here: 288 us
  waiting for transfers between devices  188 us (65%)
  matrix products  48.4 us (17%)
  starting transfers between devices  25.7 us (9%)
  between operations  14.4 us (5%)
  other arithmetic  6.41 us (2%)
  local copies, waits for them, and re-layouts  4.89 us (2%)
    ppermute x5, waiting for transfers between devices, chain_step(): lax.ppermute(value, 'col', [(2 * a + core, 2 * b + core) for a, b in move...  123 us
    ppermute x12, waiting for transfers between devices, flipped(): return lax.ppermute(value, axis, [(i, i ^ bits) for i in range(devices)])  65.7 us
    dot_general x10, matrix products, on_device(): term = jnp.dot(weights, value, preferred_element_type=jnp.float32)  29.3 us
    dot_general x5, matrix products, on_device(): lax.dot_general(piece, part, (((0,), (0,)), ((), ())), preferred_element_...  19.1 us
    ppermute x12, starting transfers between devices, flipped(): return lax.ppermute(value, axis, [(i, i ^ bits) for i in range(devices)])  13.6 us
    ppermute x5, starting transfers between devices, chain_step(): lax.ppermute(value, 'col', [(2 * a + core, 2 * b + core) for a, b in move...  12 us
  transfers between devices with their start and end apart: 19, of which 10 were waited for; matrix products, arithmetic and copies ran while one was open for 17% of the time, Pallas kernels for 0%

profile of v3, /device:TPU:0, one launch (start us, length us, event | category | flops | bytes accessed | tf_op | source)
XLA Modules:
  0.0 288.2 jit_solution(16943928283305750976)
XLA Ops:
  7.2 0.0 all-gather.3.cloned.1.call-start
  7.2 1.4 fusion.58
  8.7 0.5 collective-permute-start
  9.2 0.8 collective-permute-done
  10.0 3.0 %collective-permute-start.1 = (f32[2,768]{1,0:T(2,128)S(1)}, f32[2,768]{1,0:T(2,128)S(1)}, u32[]{:S(2)}, u32[]{:S(2)}) collective-permute-start(f32[2,768]{1,0:T(2,128)S(1)} %fusion.57), channel_id=1, source_target_pairs={{0,2},{1,3},{2,0},{3,1},{4,6},{5,7},{6,4},{7,5},{8,10},{9,11},{10,... | collective-permute-start | bytes 18440 | tf_op jit(solution)/shard_map/ppermute | solution.py:18
  13.0 1.6 collective-permute-done.1
  14.6 3.1 %collective-permute-start.2 = (f32[2,768]{1,0:T(2,128)S(1)}, f32[2,768]{1,0:T(2,128)S(1)}, u32[]{:S(2)}, u32[]{:S(2)}) collective-permute-start(f32[2,768]{1,0:T(2,128)S(1)} %fusion.74), channel_id=1, source_target_pairs={{0,4},{1,5},{2,6},{3,7},{4,0},{5,1},{6,2},{7,3},{8,12},{9,13},{10,... | collective-permute-start | bytes 18440 | tf_op jit(solution)/shard_map/ppermute | solution.py:18
  17.7 0.7 broadcast_add_fusion
  18.4 0.9 collective-permute-done.2
  19.4 2.3 add_convert_fusion
  21.7 0.0 all-gather.3.cloned.1.call-update
  21.7 0.0 all-gather.5.cloned.1.call-start
  21.8 1.9 collective-permute-start.4
  23.7 1.5 collective-permute-start.3
  25.2 48.2 %collective-permute-done.4 = bf16[768,1536]{1,0:T(8,128)(2,1)S(1)} collective-permute-done((bf16[768,1536]{1,0:T(8,128)(2,1)}, bf16[768,1536]{1,0:T(8,128)(2,1)S(1)}, u32[]{:S(2)}, u32[]{:S(2)}) %collective-permute-start.4) | collective-permute-done | bytes 2359328 | tf_op jit(solution)/shard_map/ppermute | solution.py:18
  73.3 1.1 slice.18
  74.4 1.5 collective-permute-start.5
  76.0 0.0 collective-permute-done.3
  76.0 2.4 slice.19
  78.3 1.5 collective-permute-start.6
  79.9 4.2 %fusion.28 = f32[768,1536]{1,0:T(8,128)S(1)} fusion(bf16[768,1536]{1,0:T(8,128)(2,1)} %collective-permute-done.3, bf16[3072,768]{1,0:T(8,128)(2,1)} %all-gather.3.cloned.1.call-done, s32[]{:T(128)S(6)} %select_n.73), kind=kOutput, calls=%fused_computation.37 | convolution fusion | flops 1811939328 | bytes 8257540 | tf_op jit(solution)/shard_map/dot_general | solution.py:102
  84.1 2.1 fusion.30
  86.2 4.4 %add_bitcast_fusion = f32[1536,768]{0,1:T(8,128)} fusion(f32[768,1536]{1,0:T(8,128)S(1)} %fusion.30, f32[768,1536]{1,0:T(8,128)S(1)} %fusion.28, bf16[768,1536]{1,0:T(8,128)(2,1)S(1)} %collective-permute-done.4, bf16[3072,768]{1,0:T(8,128)(2,1)S(1)} %copy-done.3, s32[]{:T(128)S(6)} %select_n.74), kind=kOutput, calls=%fused_computation.9 | convolution fusion | flops 1814298624 | bytes 17694724 | tf_op jit(solution)/shard_map/dot_general | solution.py:102
  90.6 9.4 %collective-permute-done.5 = bf16[384,1536]{1,0:T(8,128)(2,1)S(1)} collective-permute-done((bf16[384,1536]{1,0:T(8,128)(2,1)}, bf16[384,1536]{1,0:T(8,128)(2,1)S(1)}, u32[]{:S(2)}, u32[]{:S(2)}) %collective-permute-start.5) | collective-permute-done | bytes 1179680 | tf_op jit(solution)/shard_map/ppermute | solution.py:18
  99.9 3.4 %collective-permute-done.6 = bf16[384,1536]{1,0:T(8,128)(2,1)} collective-permute-done((bf16[384,1536]{1,0:T(8,128)(2,1)}, bf16[384,1536]{1,0:T(8,128)(2,1)}, u32[]{:S(2)}, u32[]{:S(2)}) %collective-permute-start.6) | collective-permute-done | bytes 1179680 | tf_op jit(solution)/shard_map/ppermute | solution.py:18
  103.3 0.0 all-gather.5.cloned.1.call-update
  103.3 0.0 slice-start.1
  103.4 0.0 copy-start.8
  103.4 2.7 fusion.36
  106.1 5.8 %fusion.7 = bf16[1536,768]{0,1:T(8,128)(2,1)} fusion(f32[1536,768]{0,1:T(8,128)S(1)} %bitcast.18, f32[1536,768]{0,1:T(8,128)S(1)} %fusion.36, f32[1536]{0:T(1024)S(1)} %copy-done.8, bf16[384,1536]{1,0:T(8,128)(2,1)} %collective-permute-done.6, bf16[3072,768]{1,0:T(8,128)(2,1)} %all-gather.3.cloned.1.call-done, s32[]{:T(128)S(6)} %select_n.76), kind=kOutput, calls=%fused_computation.8 | convolution fusion | flops 920125440 | bytes 13572100 | tf_op jit(solution)/shard_map/dot_general | solution.py:102
  111.8 1.3 collective-permute-start.9
  113.1 5.9 %collective-permute-start.7 = (bf16[1536,768]{0,1:T(8,128)(2,1)}, bf16[1536,768]{0,1:T(8,128)(2,1)}, u32[]{:S(2)}, u32[]{:S(2)}) collective-permute-start(bf16[1536,768]{0,1:T(8,128)(2,1)} %fusion.7), channel_id=1, source_target_pairs={{0,2},{1,3},{2,4},{3,5},{4,6},{5,7},{8,10},{9,11},{10,12},{11,13},... | collective-permute-start | bytes 7077896 | tf_op jit(solution)/shard_map/ppermute | solution.py:43
  119.1 44.2 %collective-permute-done.9 = bf16[1536,768]{0,1:T(8,128)(2,1)} collective-permute-done((bf16[1536,768]{0,1:T(8,128)(2,1)}, bf16[1536,768]{0,1:T(8,128)(2,1)}, u32[]{:S(2)}, u32[]{:S(2)}) %collective-permute-start.9) | collective-permute-done | bytes 2359328 | tf_op jit(solution)/shard_map/ppermute | solution.py:43
  163.2 1.3 collective-permute-start.10
  164.5 0.0 collective-permute-done.7
  164.5 2.2 collective-permute-start.8
  166.7 0.0 collective-permute-start.11
  166.7 0.5 collective-permute-start.12
  167.2 0.0 collective-permute-start.13
  167.2 46.3 %collective-permute-done.10 = bf16[1536,768]{0,1:T(8,128)(2,1)S(1)} collective-permute-done((bf16[1536,768]{0,1:T(8,128)(2,1)}, bf16[1536,768]{0,1:T(8,128)(2,1)S(1)}, u32[]{:S(2)}, u32[]{:S(2)}) %collective-permute-start.10) | collective-permute-done | bytes 2359328 | tf_op jit(solution)/shard_map/ppermute | solution.py:43
  213.5 1.4 copy-done.1
  214.9 0.0 collective-permute-done.8
  214.9 1.9 broadcast_select_fusion
  216.8 0.1 collective-permute-start.15
  217.0 0.0 collective-permute-done.11
  217.0 0.0 collective-permute-done.12
  217.0 0.0 collective-permute-done.13
  217.0 1.3 collective-permute-start.14
  218.3 0.0 all-gather.5.cloned.1.call-done
  218.3 3.3 %fusion.25 = f32[384,768]{1,0:T(8,128)S(1)} fusion(bf16[1536,768]{0,1:T(8,128)(2,1)} %fusion.7, bf16[384,12288]{1,0:T(8,128)(2,1)} %all-gather.5.cloned.1.call-done, s32[]{:T(128)S(6)} %select_n.79), kind=kOutput, calls=%fused_computation.34 | convolution fusion | flops 905969664 | bytes 4718596 | tf_op jit(solution)/shard_map/dot_general | solution.py:119
  221.6 3.6 %fusion.20 = f32[384,768]{1,0:T(8,128)S(1)} fusion(bf16[1536,768]{0,1:T(8,128)(2,1)} %collective-permute-done.9, bf16[384,12288]{1,0:T(8,128)(2,1)} %all-gather.5.cloned.1.call-done, s32[]{:T(128)S(6)} %select_n.83), kind=kOutput, calls=%fused_computation.29 | convolution fusion | flops 905969664 | bytes 4718596 | tf_op jit(solution)/shard_map/dot_general | solution.py:119
  225.2 1.1 fusion.17
  226.3 0.0 collective-permute-done.15
  226.4 2.8 fusion.15
  229.1 2.8 convolution_add_fusion.3
  231.9 2.8 convolution_add_fusion.2
  234.8 2.8 fusion.10
  237.6 2.8 fusion.9
  240.4 32.2 %collective-permute-done.14 = bf16[1536,768]{0,1:T(8,128)(2,1)} collective-permute-done((bf16[1536,768]{0,1:T(8,128)(2,1)S(1)}, bf16[1536,768]{0,1:T(8,128)(2,1)}, u32[]{:S(2)}, u32[]{:S(2)}) %collective-permute-start.14) | collective-permute-done | bytes 2359328 | tf_op jit(solution)/shard_map/ppermute | solution.py:43
  272.5 0.0 collective-permute-start.16
  272.6 0.0 copy-start.6
  272.6 3.3 %fusion.13 = f32[384,768]{1,0:T(8,128)S(1)} fusion(bf16[1536,768]{0,1:T(8,128)(2,1)} %collective-permute-done.14, bf16[384,12288]{1,0:T(8,128)(2,1)} %all-gather.5.cloned.1.call-done, s32[]{:T(128)S(6)} %select_n.89), kind=kOutput, calls=%fused_computation.22 | convolution fusion | flops 905969664 | bytes 4718596 | tf_op jit(solution)/shard_map/dot_general | solution.py:119
  275.8 1.4 collective-permute-done.16
  277.3 4.0 %multiply_add_fusion = (f32[384,768]{1,0:T(8,128)}, f32[384,768]{1,0:T(8,128)}) fusion(f32[384,768]{1,0:T(8,128)S(1)} %copy-done.2, f32[384,768]{1,0:T(8,128)S(1)} %copy-done, f32[384]{0:T(512)S(1)} %copy-done.5, bf16[1536,768]{0,1:T(8,128)(2,1)S(1)} %collective-permute-done.16, bf16[384,12288]{1,0:T(8,128)(2,1)} %all-gather.5.cloned.1.call-done, ...), kind=kOutput, calls=%fused_computation.18 | convolution fusion | flops 908918784 | bytes 10619908 | tf_op jit(solution)/shard_map/dot_general | solution.py:119
  (27 shorter events, 0.1 us)
Async XLA Ops:
  7.2 72.7 %all-gather.3.cloned.1.call-start = ((), (), s32[]{:S(2)}) async-start(), calls=%async_computation | async-start | bytes 5308416 | tf_op jit(solution)/shard_map/all_gather | solution.py:92
  8.7 1.3 collective-permute-start
  10.0 4.6 %collective-permute-start.1 = (f32[2,768]{1,0:T(2,128)S(1)}, f32[2,768]{1,0:T(2,128)S(1)}, u32[]{:S(2)}, u32[]{:S(2)}) collective-permute-start(f32[2,768]{1,0:T(2,128)S(1)} %fusion.57), channel_id=1, source_target_pairs={{0,2},{1,3},{2,0},{3,1},{4,6},{5,7},{6,4},{7,5},{8,10},{9,11},{10,... | collective-permute-start | bytes 18440 | tf_op jit(solution)/shard_map/ppermute | solution.py:18
  14.6 4.7 %collective-permute-start.2 = (f32[2,768]{1,0:T(2,128)S(1)}, f32[2,768]{1,0:T(2,128)S(1)}, u32[]{:S(2)}, u32[]{:S(2)}) collective-permute-start(f32[2,768]{1,0:T(2,128)S(1)} %fusion.74), channel_id=1, source_target_pairs={{0,4},{1,5},{2,6},{3,7},{4,0},{5,1},{6,2},{7,3},{8,12},{9,13},{10,... | collective-permute-start | bytes 18440 | tf_op jit(solution)/shard_map/ppermute | solution.py:18
  21.7 196.6 %all-gather.5.cloned.1.call-start = ((), (), s32[]{:S(2)}) async-start(), calls=%async_computation.1 | async-start | bytes 11796480 | tf_op jit(solution)/shard_map/all_gather | solution.py:108
  21.8 51.6 %collective-permute-start.4 = (bf16[768,1536]{1,0:T(8,128)(2,1)}, bf16[768,1536]{1,0:T(8,128)(2,1)S(1)}, u32[]{:S(2)}, u32[]{:S(2)}) collective-permute-start(bf16[768,1536]{1,0:T(8,128)(2,1)} %param.14), channel_id=1, source_target_pairs={{0,16},{8,24},{16,0},{24,8},{1,17},{9,25},{17,1},{25,9},{2,18},{10... | collective-permute-start | bytes 7077896 | tf_op jit(solution)/shard_map/ppermute | solution.py:18
  23.7 52.3 %collective-permute-start.3 = (bf16[768,1536]{1,0:T(8,128)(2,1)}, bf16[768,1536]{1,0:T(8,128)(2,1)}, u32[]{:S(2)}, u32[]{:S(2)}) collective-permute-start(bf16[768,1536]{1,0:T(8,128)(2,1)} %param.14), channel_id=1, source_target_pairs={{0,8},{8,0},{16,24},{24,16},{1,9},{9,1},{17,25},{25,17},{2,10},{10... | collective-permute-start | bytes 7077896 | tf_op jit(solution)/shard_map/ppermute | solution.py:18
  74.4 25.5 %collective-permute-start.5 = (bf16[384,1536]{1,0:T(8,128)(2,1)}, bf16[384,1536]{1,0:T(8,128)(2,1)S(1)}, u32[]{:S(2)}, u32[]{:S(2)}) collective-permute-start(bf16[384,1536]{1,0:T(8,128)(2,1)} %slice.18), channel_id=1, source_target_pairs={{0,8},{8,0},{16,24},{24,16},{1,9},{9,1},{17,25},{25,17},{2,10},{10... | collective-permute-start | bytes 3538952 | tf_op jit(solution)/shard_map/ppermute | solution.py:18
  78.3 25.0 %collective-permute-start.6 = (bf16[384,1536]{1,0:T(8,128)(2,1)}, bf16[384,1536]{1,0:T(8,128)(2,1)}, u32[]{:S(2)}, u32[]{:S(2)}) collective-permute-start(bf16[384,1536]{1,0:T(8,128)(2,1)} %slice.19), channel_id=1, source_target_pairs={{0,16},{8,24},{16,0},{24,8},{1,17},{9,25},{17,1},{25,9},{2,18},{10... | collective-permute-start | bytes 3538952 | tf_op jit(solution)/shard_map/ppermute | solution.py:18
  79.9 4.2 %copy-start.3 = (bf16[3072,768]{1,0:T(8,128)(2,1)S(1)}, bf16[3072,768]{1,0:T(8,128)(2,1)}, u32[]{:S(2)}) copy-start(bf16[3072,768]{1,0:T(8,128)(2,1)} %all-gather.3.cloned.1.call-done) | copy-start | bytes 14155780
  79.9 4.2 %copy-start.7 = (bf16[768,1536]{1,0:T(8,128)(2,1)S(1)}, bf16[768,1536]{1,0:T(8,128)(2,1)}, u32[]{:S(2)}) copy-start(bf16[768,1536]{1,0:T(8,128)(2,1)} %param.14) | copy-start | bytes 7077892
  103.3 2.7 slice-start
  103.3 2.7 slice-start.1
  103.4 2.7 copy-start.8
  111.8 51.4 %collective-permute-start.9 = (bf16[1536,768]{0,1:T(8,128)(2,1)}, bf16[1536,768]{0,1:T(8,128)(2,1)}, u32[]{:S(2)}, u32[]{:S(2)}) collective-permute-start(bf16[1536,768]{0,1:T(8,128)(2,1)} %fusion.7), channel_id=1, source_target_pairs={{2,0},{3,1},{4,2},{5,3},{6,4},{7,5},{10,8},{11,9},{12,10},{13,11},... | collective-permute-start | bytes 7077896 | tf_op jit(solution)/shard_map/ppermute | solution.py:43
  113.1 51.4 %collective-permute-start.7 = (bf16[1536,768]{0,1:T(8,128)(2,1)}, bf16[1536,768]{0,1:T(8,128)(2,1)}, u32[]{:S(2)}, u32[]{:S(2)}) collective-permute-start(bf16[1536,768]{0,1:T(8,128)(2,1)} %fusion.7), channel_id=1, source_target_pairs={{0,2},{1,3},{2,4},{3,5},{4,6},{5,7},{8,10},{9,11},{10,12},{11,13},... | collective-permute-start | bytes 7077896 | tf_op jit(solution)/shard_map/ppermute | solution.py:43
  163.2 50.2 %collective-permute-start.10 = (bf16[1536,768]{0,1:T(8,128)(2,1)}, bf16[1536,768]{0,1:T(8,128)(2,1)S(1)}, u32[]{:S(2)}, u32[]{:S(2)}) collective-permute-start(bf16[1536,768]{0,1:T(8,128)(2,1)} %collective-permute-done.9), channel_id=1, source_target_pairs={{2,0},{3,1},{4,2},{5,3},{10,8},{11,9},{12,10},{13,11},{18,16},{19,... | collective-permute-start | bytes 7077896 | tf_op jit(solution)/shard_map/ppermute | solution.py:43
  164.5 50.3 %collective-permute-start.8 = (bf16[1536,768]{0,1:T(8,128)(2,1)}, bf16[1536,768]{0,1:T(8,128)(2,1)}, u32[]{:S(2)}, u32[]{:S(2)}) collective-permute-start(bf16[1536,768]{0,1:T(8,128)(2,1)} %collective-permute-done.7), channel_id=1, source_target_pairs={{2,4},{3,5},{4,6},{5,7},{10,12},{11,13},{12,14},{13,15},{18,20},{1... | collective-permute-start | bytes 7077896 | tf_op jit(solution)/shard_map/ppermute | solution.py:43
  166.7 50.3 %collective-permute-start.11 = (bf16[1536,768]{0,1:T(8,128)(2,1)}, bf16[1536,768]{0,1:T(8,128)(2,1)}, u32[]{:S(2)}, u32[]{:S(2)}) collective-permute-start(bf16[1536,768]{0,1:T(8,128)(2,1)} %fusion.7), channel_id=1, source_target_pairs={{0,1},{1,0},{2,3},{3,2},{4,5},{5,4},{6,7},{7,6},{8,9},{9,8},{10,11... | collective-permute-start | bytes 7077896 | tf_op jit(solution)/shard_map/ppermute | solution.py:18
  166.7 50.3 %collective-permute-start.12 = (bf16[1536,768]{0,1:T(8,128)(2,1)}, bf16[1536,768]{0,1:T(8,128)(2,1)}, u32[]{:S(2)}, u32[]{:S(2)}) collective-permute-start(bf16[1536,768]{0,1:T(8,128)(2,1)} %collective-permute-done.7), channel_id=1, source_target_pairs={{0,1},{1,0},{2,3},{3,2},{4,5},{5,4},{6,7},{7,6},{8,9},{9,8},{10,11... | collective-permute-start | bytes 7077896 | tf_op jit(solution)/shard_map/ppermute | solution.py:18
  167.2 49.8 %collective-permute-start.13 = (bf16[1536,768]{0,1:T(8,128)(2,1)}, bf16[1536,768]{0,1:T(8,128)(2,1)}, u32[]{:S(2)}, u32[]{:S(2)}) collective-permute-start(bf16[1536,768]{0,1:T(8,128)(2,1)} %collective-permute-done.9), channel_id=1, source_target_pairs={{0,1},{1,0},{2,3},{3,2},{4,5},{5,4},{6,7},{7,6},{8,9},{9,8},{10,11... | collective-permute-start | bytes 7077896 | tf_op jit(solution)/shard_map/ppermute | solution.py:18
  213.5 1.4 copy-start.1
  216.8 9.6 %collective-permute-start.15 = (bf16[1536,768]{0,1:T(8,128)(2,1)S(1)}, bf16[1536,768]{0,1:T(8,128)(2,1)}, u32[]{:S(2)}, u32[]{:S(2)}) collective-permute-start(bf16[1536,768]{0,1:T(8,128)(2,1)S(1)} %broadcast_select_fusion), channel_id=1, source_target_pairs={{0,1},{1,0},{2,3},{3,2},{4,5},{5,4},{6,7},{7,6},{8,9},{9,8},{10,11... | collective-permute-start | bytes 7077896 | tf_op jit(solution)/shard_map/ppermute | solution.py:18
  217.0 55.5 %collective-permute-start.14 = (bf16[1536,768]{0,1:T(8,128)(2,1)S(1)}, bf16[1536,768]{0,1:T(8,128)(2,1)}, u32[]{:S(2)}, u32[]{:S(2)}) collective-permute-start(bf16[1536,768]{0,1:T(8,128)(2,1)S(1)} %broadcast_select_fusion), channel_id=1, source_target_pairs={{4,6},{5,7},{2,0},{3,1},{12,14},{13,15},{10,8},{11,9},{20,22},{21,... | collective-permute-start | bytes 7077896 | tf_op jit(solution)/shard_map/ppermute | solution.py:43
  218.3 6.9 %copy-start.4 = (bf16[384,12288]{1,0:T(8,128)(2,1)S(1)}, bf16[384,12288]{1,0:T(8,128)(2,1)}, u32[]{:S(2)}) copy-start(bf16[384,12288]{1,0:T(8,128)(2,1)} %all-gather.5.cloned.1.call-done) | copy-start | bytes 28311556
  272.5 4.7 %collective-permute-start.16 = (bf16[1536,768]{0,1:T(8,128)(2,1)}, bf16[1536,768]{0,1:T(8,128)(2,1)S(1)}, u32[]{:S(2)}, u32[]{:S(2)}) collective-permute-start(bf16[1536,768]{0,1:T(8,128)(2,1)} %collective-permute-done.14), channel_id=1, source_target_pairs={{0,1},{1,0},{2,3},{3,2},{4,5},{5,4},{6,7},{7,6},{8,9},{9,8},{10,11... | collective-permute-start | bytes 7077896 | tf_op jit(solution)/shard_map/ppermute | solution.py:18
  272.5 4.7 %copy-start = (f32[384,768]{1,0:T(8,128)S(1)}, f32[384,768]{1,0:T(8,128)}, u32[]{:S(2)}) copy-start(f32[384,768]{1,0:T(8,128)} %param.9) | copy-start | bytes 3538948
  272.5 4.7 %copy-start.2 = (f32[384,768]{1,0:T(8,128)S(1)}, f32[384,768]{1,0:T(8,128)}, u32[]{:S(2)}) copy-start(f32[384,768]{1,0:T(8,128)} %param.10) | copy-start | bytes 3538948
  272.5 4.7 %copy-start.5 = (f32[384]{0:T(512)S(1)}, f32[384]{0:T(512)}, u32[]{:S(2)}) copy-start(f32[384]{0:T(512)} %param.17) | copy-start | bytes 4612
  272.6 4.7 %copy-start.6 = (f32[384]{0:T(512)S(1)}, f32[384]{0:T(512)}, u32[]{:S(2)}) copy-start(f32[384]{0:T(512)} %param.13) | copy-start | bytes 4612
Sparse Core Ops, SparseCore 0:
  21.8 53.2 all-gather.2
  103.5 96.6 all-gather.4

commit v4 on v3

--- a/solution.py
+++ b/solution.py
@@ -91,33 +91,42 @@
     ).astype(jnp.bfloat16)
     normed_all = lax.all_gather(normed, "col", axis=0, tiled=True)
 
-    pre_act = None
-    for k, parts in in_pieces.items():
-        if k and len(parts) > 1:
-            pre_act, *arrived = lax.optimization_barrier((pre_act, *[piece for _, piece in parts]))
-            parts = [(offset, piece) for (offset, _), piece in zip(parts, arrived)]
-        for offset, piece in parts:
-            start = (row ^ k) * w_in.shape[0] + offset
-            part = lax.dynamic_slice_in_dim(normed_all, start, piece.shape[0], axis=0)
-            term = lax.dot_general(
-                piece, part, (((0,), (0,)), ((), ())), preferred_element_type=jnp.float32
-            )
-            pre_act = term if pre_act is None else pre_act + term
-    hidden = jax.nn.gelu(pre_act + b_in[:, None], approximate=True).astype(jnp.bfloat16)
+    tokens = state.shape[1]
+    spans = [(0, tokens // 2), (tokens // 2, tokens)]
+    chains = []
+    for lo, hi in spans:
+        pre_act = None
+        for k, parts in in_pieces.items():
+            if k and len(parts) > 1:
+                pre_act, *arrived = lax.optimization_barrier((pre_act, *[piece for _, piece in parts]))
+                parts = [(offset, piece) for (offset, _), piece in zip(parts, arrived)]
+            for offset, piece in parts:
+                start = (row ^ k) * w_in.shape[0] + offset
+                part = lax.dynamic_slice(normed_all, (start, lo), (piece.shape[0], hi - lo))
+                term = lax.dot_general(
+                    piece, part, (((0,), (0,)), ((), ())), preferred_element_type=jnp.float32
+                )
+                pre_act = term if pre_act is None else pre_act + term
+        hidden = jax.nn.gelu(pre_act + b_in[:, None], approximate=True).astype(jnp.bfloat16)
+        chains.append(gather_chain(hidden))
     w_out, _ = lax.optimization_barrier((w_out, piece))
     w_out_all = lax.all_gather(w_out, "row", axis=1, tiled=True)
 
-    mixed_out = None
-    units = w_in.shape[1]
-    blocks = gather_chain(hidden)
-    for owner, block, swapped in blocks:
-        if swapped is None:
-            block, mixed_out = lax.optimization_barrier((block, mixed_out))
-            swapped = flipped(block, "col", 1)
-        for near, value in ((core, block), (1 - core, swapped)):
-            weights = lax.dynamic_slice_in_dim(w_out_all, (2 * owner + near) * units, units, axis=1)
-            term = jnp.dot(weights, value, preferred_element_type=jnp.float32)
-            mixed_out = term if mixed_out is None else mixed_out + term
+
+    halves = []
+    for blocks in chains:
+        mixed_out = None
+        units = w_in.shape[1]
+        for owner, block, swapped in blocks:
+            if swapped is None:
+                block, mixed_out = lax.optimization_barrier((block, mixed_out))
+                swapped = flipped(block, "col", 1)
+            for near, value in ((core, block), (1 - core, swapped)):
+                weights = lax.dynamic_slice_in_dim(w_out_all, (2 * owner + near) * units, units, axis=1)
+                term = jnp.dot(weights, value, preferred_element_type=jnp.float32)
+                mixed_out = term if mixed_out is None else mixed_out + term
+        halves.append(mixed_out)
+    mixed_out = lax.concatenate(halves, 1)
     branch = mixed_out + b_out[:, None]
     predicted = state + mod_gate[:, None] * branch
     purified = (

time: 290 us -> 290 us (level)
  waiting for transfers between devices: 188 us -> 159 us
  matrix products: 48.4 us -> 65.5 us
  starting transfers between devices: 25.7 us -> 35.7 us
    ppermute x5 -> x10, waiting for transfers between devices: 123 us -> 92.2 us  [chain_step(): lax.ppermute(value, 'col', [(2 * a + core, 2 * b + core) for a, b in move...]
    dot_general x10 -> x20, matrix products: 29.3 us -> 39.2 us  [on_device(): term = jnp.dot(weights, value, preferred_element_type=jnp.float32)]
    ppermute x5 -> x10, starting transfers between devices: 12 us -> 20.5 us  [chain_step(): lax.ppermute(value, 'col', [(2 * a + core, 2 * b + core) for a, b in move...]
    dot_general x5 -> x10, matrix products: 19.1 us -> 26.3 us  [on_device(): lax.dot_general(piece, part, (((0,), (0,)), ((), ())), preferred_element_...]
    ppermute x12 -> x17, starting transfers between devices: 13.6 us -> 15.1 us  [flipped(): return lax.ppermute(value, axis, [(i, i ^ bits) for i in range(devices)])]
    ppermute x12 -> x17, waiting for transfers between devices: 65.7 us -> 66.6 us  [flipped(): return lax.ppermute(value, axis, [(i, i ^ bits) for i in range(devices)])]
  transfers between devices with their start and end apart: 19 -> 29, of which waited for: 10 -> 13; matrix products, arithmetic and copies ran while one was open for 17% -> 24% of each run, Pallas kernels for 0% -> 0%
where the time goes in v4:
time: 290 us; the launch traced here: 289 us
  waiting for transfers between devices  159 us (55%)
  matrix products  65.5 us (23%)
  starting transfers between devices  35.7 us (12%)
  between operations  14.7 us (5%)
  other arithmetic  8.1 us (3%)
  local copies, waits for them, and re-layouts  5.63 us (2%)
    ppermute x10, waiting for transfers between devices, chain_step(): lax.ppermute(value, 'col', [(2 * a + core, 2 * b + core) for a, b in move...  92.2 us
    ppermute x17, waiting for transfers between devices, flipped(): return lax.ppermute(value, axis, [(i, i ^ bits) for i in range(devices)])  66.6 us
    dot_general x20, matrix products, on_device(): term = jnp.dot(weights, value, preferred_element_type=jnp.float32)  39.2 us
    dot_general x10, matrix products, on_device(): lax.dot_general(piece, part, (((0,), (0,)), ((), ())), preferred_element_...  26.3 us
    ppermute x10, starting transfers between devices, chain_step(): lax.ppermute(value, 'col', [(2 * a + core, 2 * b + core) for a, b in move...  20.5 us
    ppermute x17, starting transfers between devices, flipped(): return lax.ppermute(value, axis, [(i, i ^ bits) for i in range(devices)])  15.1 us
  transfers between devices with their start and end apart: 29, of which 13 were waited for; matrix products, arithmetic and copies ran while one was open for 24% of the time, Pallas kernels for 0%

profile of v4, /device:TPU:0, one launch (start us, length us, event | category | flops | bytes accessed | tf_op | source)
XLA Modules:
  0.0 288.5 jit_solution(11139310056057260159)
XLA Ops:
  7.2 1.5 fusion.115
  9.3 0.8 collective-permute-done
  10.1 3.0 %collective-permute-start.1 = (f32[2,768]{1,0:T(2,128)S(1)}, f32[2,768]{1,0:T(2,128)S(1)}, u32[]{:S(2)}, u32[]{:S(2)}) collective-permute-start(f32[2,768]{1,0:T(2,128)S(1)} %fusion.114), channel_id=1, source_target_pairs={{0,2},{1,3},{2,0},{3,1},{4,6},{5,7},{6,4},{7,5},{8,10},{9,11},{10,... | collective-permute-start | bytes 18440 | tf_op jit(solution)/shard_map/ppermute | solution.py:18
  13.1 1.6 collective-permute-done.1
  14.7 3.1 %collective-permute-start.2 = (f32[2,768]{1,0:T(2,128)S(1)}, f32[2,768]{1,0:T(2,128)S(1)}, u32[]{:S(2)}, u32[]{:S(2)}) collective-permute-start(f32[2,768]{1,0:T(2,128)S(1)} %fusion.147), channel_id=1, source_target_pairs={{0,4},{1,5},{2,6},{3,7},{4,0},{5,1},{6,2},{7,3},{8,12},{9,13},{10,... | collective-permute-start | bytes 18440 | tf_op jit(solution)/shard_map/ppermute | solution.py:18
  17.8 1.6 collective-permute-done.2
  19.5 1.0 add_convert_fusion
  20.6 1.9 collective-permute-start.3
  22.5 1.5 collective-permute-start.4
  24.0 48.2 %collective-permute-done.3 = bf16[768,1536]{1,0:T(8,128)(2,1)S(1)} collective-permute-done((bf16[768,1536]{1,0:T(8,128)(2,1)}, bf16[768,1536]{1,0:T(8,128)(2,1)S(1)}, u32[]{:S(2)}, u32[]{:S(2)}) %collective-permute-start.3) | collective-permute-done | bytes 2359328 | tf_op jit(solution)/shard_map/ppermute | solution.py:18
  72.2 1.1 slice.19
  73.3 1.6 collective-permute-start.6
  74.9 1.4 copy-done.1
  76.3 1.1 slice.18
  77.4 1.5 collective-permute-start.5
  78.8 3.0 %fusion.60 = f32[384,1536]{1,0:T(8,128)S(1)} fusion(bf16[768,1536]{1,0:T(8,128)(2,1)} %param.14, bf16[3072,768]{1,0:T(8,128)(2,1)} %all-gather.3.cloned.1.call-done, s32[]{:T(128)S(6)} %select_n.94), kind=kOutput, calls=%fused_computation.82 | convolution fusion | flops 905969664 | bytes 5308420 | tf_op jit(solution)/shard_map/dot_general | solution.py:106
  81.8 2.3 convolution_add_fusion.1
  84.2 3.6 %fusion.1 = f32[1536,384]{0,1:T(8,128)} fusion(f32[384,1536]{1,0:T(8,128)S(1)} %convolution_add_fusion.1, bf16[768,1536]{1,0:T(8,128)(2,1)S(1)} %copy-done.2, bf16[3072,768]{1,0:T(8,128)(2,1)} %all-gather.3.cloned.1.call-done, s32[]{:T(128)S(6)} %select_n.96), kind=kOutput, calls=%fused_computation.7 | convolution fusion | flops 906559488 | bytes 7667716 | tf_op jit(solution)/shard_map/dot_general | solution.py:106
  87.8 11.0 %collective-permute-done.6 = bf16[384,1536]{1,0:T(8,128)(2,1)} collective-permute-done((bf16[384,1536]{1,0:T(8,128)(2,1)}, bf16[384,1536]{1,0:T(8,128)(2,1)}, u32[]{:S(2)}, u32[]{:S(2)}) %collective-permute-start.6) | collective-permute-done | bytes 1179680 | tf_op jit(solution)/shard_map/ppermute | solution.py:18
  98.8 3.4 %collective-permute-done.5 = bf16[384,1536]{1,0:T(8,128)(2,1)S(1)} collective-permute-done((bf16[384,1536]{1,0:T(8,128)(2,1)}, bf16[384,1536]{1,0:T(8,128)(2,1)S(1)}, u32[]{:S(2)}, u32[]{:S(2)}) %collective-permute-start.5) | collective-permute-done | bytes 1179680 | tf_op jit(solution)/shard_map/ppermute | solution.py:18
  102.3 1.9 fusion.70
  104.2 3.0 %fusion.17 = bf16[1536,384]{0,1:T(8,128)(2,1)S(1)} fusion(f32[1536,384]{0,1:T(8,128)S(1)} %copy-done.7, f32[1536,384]{0,1:T(8,128)S(1)} %fusion.70, f32[1536]{0:T(1024)S(1)} %copy-done.22, bf16[384,1536]{1,0:T(8,128)(2,1)} %collective-permute-done.6, bf16[3072,768]{1,0:T(8,128)(2,1)} %all-gather.3.cloned.1.call-done, s32[]{:T(128)S(6)} %select_n.98), kind=kOutput, calls=%fused_computation.23 | convolution fusion | flops 460062720 | bytes 7378948 | tf_op jit(solution)/shard_map/dot_general | solution.py:106
  107.3 1.3 collective-permute-start.19
  108.6 4.6 %collective-permute-start.17 = (bf16[1536,384]{0,1:T(8,128)(2,1)S(1)}, bf16[1536,384]{0,1:T(8,128)(2,1)S(1)}, u32[]{:S(2)}, u32[]{:S(2)}) collective-permute-start(bf16[1536,384]{0,1:T(8,128)(2,1)S(1)} %fusion.17), channel_id=1, source_target_pairs={{0,2},{1,3},{2,4},{3,5},{4,6},{5,7},{8,10},{9,11},{10,12},{11,13},... | collective-permute-start | bytes 3538952 | tf_op jit(solution)/shard_map/ppermute | solution.py:43
  113.3 2.3 fusion.64
  115.6 2.3 convolution_add_fusion.3
  117.9 2.2 fusion
  120.1 1.8 fusion.76
  121.9 3.9 %fusion.9 = bf16[1536,384]{0,1:T(8,128)(2,1)} fusion(f32[1536,384]{0,1:T(8,128)S(1)} %fusion, f32[1536,384]{0,1:T(8,128)S(1)} %fusion.76, f32[1536]{0:T(1024)S(1)} %copy-done.22, bf16[384,1536]{1,0:T(8,128)(2,1)} %collective-permute-done.6, bf16[3072,768]{1,0:T(8,128)(2,1)} %all-gather.3.cloned.1.call-done, s32[]{:T(128)S(6)} %select_n.98), kind=kOutput, calls=%fused_computation.15 | convolution fusion | flops 460062720 | bytes 7378948 | tf_op jit(solution)/shard_map/dot_general | solution.py:106
  125.8 1.3 collective-permute-start.9
  127.1 5.6 %collective-permute-start.7 = (bf16[1536,384]{0,1:T(8,128)(2,1)}, bf16[1536,384]{0,1:T(8,128)(2,1)}, u32[]{:S(2)}, u32[]{:S(2)}) collective-permute-start(bf16[1536,384]{0,1:T(8,128)(2,1)} %fusion.9), channel_id=1, source_target_pairs={{0,2},{1,3},{2,4},{3,5},{4,6},{5,7},{8,10},{9,11},{10,12},{11,13},... | collective-permute-start | bytes 3538952 | tf_op jit(solution)/shard_map/ppermute | solution.py:43
  132.7 5.3 %collective-permute-done.19 = bf16[1536,384]{0,1:T(8,128)(2,1)S(1)} collective-permute-done((bf16[1536,384]{0,1:T(8,128)(2,1)S(1)}, bf16[1536,384]{0,1:T(8,128)(2,1)S(1)}, u32[]{:S(2)}, u32[]{:S(2)}) %collective-permute-start.19) | collective-permute-done | bytes 1179680 | tf_op jit(solution)/shard_map/ppermute | solution.py:43
  138.0 1.3 collective-permute-start.20
  139.9 23.5 %collective-permute-done.9 = bf16[1536,384]{0,1:T(8,128)(2,1)} collective-permute-done((bf16[1536,384]{0,1:T(8,128)(2,1)}, bf16[1536,384]{0,1:T(8,128)(2,1)}, u32[]{:S(2)}, u32[]{:S(2)}) %collective-permute-start.9) | collective-permute-done | bytes 1179680 | tf_op jit(solution)/shard_map/ppermute | solution.py:43
  164.1 1.3 collective-permute-start.10
  165.4 1.7 collective-permute-start.8
  167.1 21.4 %collective-permute-done.20 = bf16[1536,384]{0,1:T(8,128)(2,1)S(1)} collective-permute-done((bf16[1536,384]{0,1:T(8,128)(2,1)S(1)}, bf16[1536,384]{0,1:T(8,128)(2,1)S(1)}, u32[]{:S(2)}, u32[]{:S(2)}) %collective-permute-start.20) | collective-permute-done | bytes 1179680 | tf_op jit(solution)/shard_map/ppermute | solution.py:43
  189.6 1.0 copy-done.15
  191.1 1.1 broadcast_select_fusion
  192.3 21.2 %collective-permute-done.10 = bf16[1536,384]{0,1:T(8,128)(2,1)} collective-permute-done((bf16[1536,384]{0,1:T(8,128)(2,1)}, bf16[1536,384]{0,1:T(8,128)(2,1)}, u32[]{:S(2)}, u32[]{:S(2)}) %collective-permute-start.10) | collective-permute-done | bytes 1179680 | tf_op jit(solution)/shard_map/ppermute | solution.py:43
  213.5 1.3 collective-permute-start.24
  214.8 2.5 broadcast_select_fusion.1
  217.9 1.5 collective-permute-start.14
  219.4 2.6 fusion.54
  221.9 3.0 %fusion.44 = f32[384,384]{1,0:T(8,128)S(1)} fusion(bf16[1536,384]{0,1:T(8,128)(2,1)} %copy-done.21, bf16[384,12288]{1,0:T(8,128)(2,1)} %all-gather.5.cloned.1.call-done, s32[]{:T(128)S(6)} %select_n.105), kind=kOutput, calls=%fused_computation.64 | convolution fusion | flops 452984832 | bytes 2949124 | tf_op jit(solution)/shard_map/dot_general | solution.py:126
  224.9 2.1 convolution_add_fusion.7
  227.0 2.2 fusion.38
  231.3 2.1 fusion.34
  233.4 0.8 fusion.19
  234.2 12.6 %collective-permute-done.24 = bf16[1536,384]{0,1:T(8,128)(2,1)} collective-permute-done((bf16[1536,384]{0,1:T(8,128)(2,1)}, bf16[1536,384]{0,1:T(8,128)(2,1)}, u32[]{:S(2)}, u32[]{:S(2)}) %collective-permute-start.24) | collective-permute-done | bytes 1179680 | tf_op jit(solution)/shard_map/ppermute | solution.py:43
  246.8 2.1 fusion.56
  248.9 2.1 fusion.46
  251.0 2.1 fusion.40
  253.1 2.1 fusion.36
  255.1 2.1 convolution_add_fusion.11
  257.2 2.1 convolution_add_fusion.10
  259.3 2.1 fusion.23
  261.4 0.9 fusion.22
  262.3 7.9 %collective-permute-done.14 = bf16[1536,384]{0,1:T(8,128)(2,1)} collective-permute-done((bf16[1536,384]{0,1:T(8,128)(2,1)}, bf16[1536,384]{0,1:T(8,128)(2,1)}, u32[]{:S(2)}, u32[]{:S(2)}) %collective-permute-start.14) | collective-permute-done | bytes 1179680 | tf_op jit(solution)/shard_map/ppermute | solution.py:43
  270.2 2.4 fusion.30
  272.6 2.4 fusion.32
  275.0 2.4 add_add_fusion
  277.6 2.2 add_add_fusion.1
  279.9 1.8 multiply_add_fusion
  (87 shorter events, 6.4 us)
Async XLA Ops:
  7.2 12.3 %copy-start.4 = (f32[384,768]{1,0:T(8,128)S(1)}, f32[384,768]{1,0:T(8,128)}, u32[]{:S(2)}) copy-start(f32[384,768]{1,0:T(8,128)} %param.9) | copy-start | bytes 3538948
  7.2 10.7 %copy-start.19 = (f32[384]{0:T(512)S(1)}, f32[384]{0:T(512)}, u32[]{:S(2)}) copy-start(f32[384]{0:T(512)} %param.12) | copy-start | bytes 4612
  7.2 12.3 %copy-start.18 = (f32[384]{0:T(512)S(1)}, f32[384]{0:T(512)}, u32[]{:S(2)}) copy-start(f32[384]{0:T(512)} %param.11) | copy-start | bytes 4612
  7.2 71.7 %all-gather.3.cloned.1.call-start = ((), (), s32[]{:S(2)}) async-start(), calls=%async_computation | async-start | bytes 5308416 | tf_op jit(solution)/shard_map/all_gather | solution.py:92
  8.8 1.3 collective-permute-start
  10.1 4.6 %collective-permute-start.1 = (f32[2,768]{1,0:T(2,128)S(1)}, f32[2,768]{1,0:T(2,128)S(1)}, u32[]{:S(2)}, u32[]{:S(2)}) collective-permute-start(f32[2,768]{1,0:T(2,128)S(1)} %fusion.114), channel_id=1, source_target_pairs={{0,2},{1,3},{2,0},{3,1},{4,6},{5,7},{6,4},{7,5},{8,10},{9,11},{10,... | collective-permute-start | bytes 18440 | tf_op jit(solution)/shard_map/ppermute | solution.py:18
  14.7 4.7 %collective-permute-start.2 = (f32[2,768]{1,0:T(2,128)S(1)}, f32[2,768]{1,0:T(2,128)S(1)}, u32[]{:S(2)}, u32[]{:S(2)}) collective-permute-start(f32[2,768]{1,0:T(2,128)S(1)} %fusion.147), channel_id=1, source_target_pairs={{0,4},{1,5},{2,6},{3,7},{4,0},{5,1},{6,2},{7,3},{8,12},{9,13},{10,... | collective-permute-start | bytes 18440 | tf_op jit(solution)/shard_map/ppermute | solution.py:18
  20.6 198.8 %all-gather.5.cloned.1.call-start = ((), (), s32[]{:S(2)}) async-start(), calls=%async_computation.1 | async-start | bytes 11796480 | tf_op jit(solution)/shard_map/all_gather | solution.py:113
  20.6 51.6 %collective-permute-start.3 = (bf16[768,1536]{1,0:T(8,128)(2,1)}, bf16[768,1536]{1,0:T(8,128)(2,1)S(1)}, u32[]{:S(2)}, u32[]{:S(2)}) collective-permute-start(bf16[768,1536]{1,0:T(8,128)(2,1)} %param.14), channel_id=1, source_target_pairs={{0,8},{8,0},{16,24},{24,16},{1,9},{9,1},{17,25},{25,17},{2,10},{10... | collective-permute-start | bytes 7077896 | tf_op jit(solution)/shard_map/ppermute | solution.py:18
  22.5 52.4 %collective-permute-start.4 = (bf16[768,1536]{1,0:T(8,128)(2,1)}, bf16[768,1536]{1,0:T(8,128)(2,1)S(1)}, u32[]{:S(2)}, u32[]{:S(2)}) collective-permute-start(bf16[768,1536]{1,0:T(8,128)(2,1)} %param.14), channel_id=1, source_target_pairs={{0,16},{8,24},{16,0},{24,8},{1,17},{9,25},{17,1},{25,9},{2,18},{10... | collective-permute-start | bytes 7077896 | tf_op jit(solution)/shard_map/ppermute | solution.py:18
  73.3 25.6 %collective-permute-start.6 = (bf16[384,1536]{1,0:T(8,128)(2,1)}, bf16[384,1536]{1,0:T(8,128)(2,1)}, u32[]{:S(2)}, u32[]{:S(2)}) collective-permute-start(bf16[384,1536]{1,0:T(8,128)(2,1)} %slice.19), channel_id=1, source_target_pairs={{0,16},{8,24},{16,0},{24,8},{1,17},{9,25},{17,1},{25,9},{2,18},{10... | collective-permute-start | bytes 3538952 | tf_op jit(solution)/shard_map/ppermute | solution.py:18
  74.9 1.4 copy-start.1
  77.4 24.9 %collective-permute-start.5 = (bf16[384,1536]{1,0:T(8,128)(2,1)}, bf16[384,1536]{1,0:T(8,128)(2,1)S(1)}, u32[]{:S(2)}, u32[]{:S(2)}) collective-permute-start(bf16[384,1536]{1,0:T(8,128)(2,1)} %slice.18), channel_id=1, source_target_pairs={{0,8},{8,0},{16,24},{24,16},{1,9},{9,1},{17,25},{25,17},{2,10},{10... | collective-permute-start | bytes 3538952 | tf_op jit(solution)/shard_map/ppermute | solution.py:18
  81.8 2.4 copy-start.2
  102.2 2.0 copy-start.7
  102.3 2.0 copy-start.22
  104.2 9.0 %copy-start.6 = (bf16[768,1536]{1,0:T(8,128)(2,1)S(1)}, bf16[768,1536]{1,0:T(8,128)(2,1)}, u32[]{:S(2)}) copy-start(bf16[768,1536]{1,0:T(8,128)(2,1)} %param.14) | copy-start | bytes 7077892
  107.2 8.4 %copy-start.20 = (bf16[1536,384]{0,1:T(8,128)(2,1)}, bf16[1536,384]{0,1:T(8,128)(2,1)S(1)}, u32[]{:S(2)}) copy-start(bf16[1536,384]{0,1:T(8,128)(2,1)S(1)} %fusion.17) | copy-start | bytes 3538948
  107.2 30.7 %collective-permute-start.21 = (bf16[1536,384]{0,1:T(8,128)(2,1)S(1)}, bf16[1536,384]{0,1:T(8,128)(2,1)S(1)}, u32[]{:S(2)}, u32[]{:S(2)}) collective-permute-start(bf16[1536,384]{0,1:T(8,128)(2,1)S(1)} %fusion.17), channel_id=1, source_target_pairs={{0,1},{1,0},{2,3},{3,2},{4,5},{5,4},{6,7},{7,6},{8,9},{9,8},{10,11... | collective-permute-start | bytes 3538952 | tf_op jit(solution)/shard_map/ppermute | solution.py:18
  107.3 30.7 %collective-permute-start.19 = (bf16[1536,384]{0,1:T(8,128)(2,1)S(1)}, bf16[1536,384]{0,1:T(8,128)(2,1)S(1)}, u32[]{:S(2)}, u32[]{:S(2)}) collective-permute-start(bf16[1536,384]{0,1:T(8,128)(2,1)S(1)} %fusion.17), channel_id=1, source_target_pairs={{2,0},{3,1},{4,2},{5,3},{6,4},{7,5},{10,8},{11,9},{12,10},{13,11},... | collective-permute-start | bytes 3538952 | tf_op jit(solution)/shard_map/ppermute | solution.py:43
  108.6 30.9 %collective-permute-start.17 = (bf16[1536,384]{0,1:T(8,128)(2,1)S(1)}, bf16[1536,384]{0,1:T(8,128)(2,1)S(1)}, u32[]{:S(2)}, u32[]{:S(2)}) collective-permute-start(bf16[1536,384]{0,1:T(8,128)(2,1)S(1)} %fusion.17), channel_id=1, source_target_pairs={{0,2},{1,3},{2,4},{3,5},{4,6},{5,7},{8,10},{9,11},{10,12},{11,13},... | collective-permute-start | bytes 3538952 | tf_op jit(solution)/shard_map/ppermute | solution.py:43
  115.6 2.3 copy-start.3
  125.8 37.6 %collective-permute-start.9 = (bf16[1536,384]{0,1:T(8,128)(2,1)}, bf16[1536,384]{0,1:T(8,128)(2,1)}, u32[]{:S(2)}, u32[]{:S(2)}) collective-permute-start(bf16[1536,384]{0,1:T(8,128)(2,1)} %fusion.9), channel_id=1, source_target_pairs={{2,0},{3,1},{4,2},{5,3},{6,4},{7,5},{10,8},{11,9},{12,10},{13,11},... | collective-permute-start | bytes 3538952 | tf_op jit(solution)/shard_map/ppermute | solution.py:43
  127.1 37.0 %collective-permute-start.7 = (bf16[1536,384]{0,1:T(8,128)(2,1)}, bf16[1536,384]{0,1:T(8,128)(2,1)}, u32[]{:S(2)}, u32[]{:S(2)}) collective-permute-start(bf16[1536,384]{0,1:T(8,128)(2,1)} %fusion.9), channel_id=1, source_target_pairs={{0,2},{1,3},{2,4},{3,5},{4,6},{5,7},{8,10},{9,11},{10,12},{11,13},... | collective-permute-start | bytes 3538952 | tf_op jit(solution)/shard_map/ppermute | solution.py:43
  138.0 51.2 %copy-start.21 = (bf16[1536,384]{0,1:T(8,128)(2,1)}, bf16[1536,384]{0,1:T(8,128)(2,1)S(1)}, u32[]{:S(2)}) copy-start(bf16[1536,384]{0,1:T(8,128)(2,1)S(1)} %collective-permute-done.19) | copy-start | bytes 3538948
  138.0 27.4 %collective-permute-start.23 = (bf16[1536,384]{0,1:T(8,128)(2,1)S(1)}, bf16[1536,384]{0,1:T(8,128)(2,1)S(1)}, u32[]{:S(2)}, u32[]{:S(2)}) collective-permute-start(bf16[1536,384]{0,1:T(8,128)(2,1)S(1)} %collective-permute-done.19), channel_id=1, source_target_pairs={{0,1},{1,0},{2,3},{3,2},{4,5},{5,4},{6,7},{7,6},{8,9},{9,8},{10,11... | collective-permute-start | bytes 3538952 | tf_op jit(solution)/shard_map/ppermute | solution.py:18
  138.0 50.6 %copy-start.9 = (bf16[1536,384]{0,1:T(8,128)(2,1)}, bf16[1536,384]{0,1:T(8,128)(2,1)S(1)}, u32[]{:S(2)}) copy-start(bf16[1536,384]{0,1:T(8,128)(2,1)S(1)} %collective-permute-done.21) | copy-start | bytes 3538948
  138.0 50.5 %collective-permute-start.20 = (bf16[1536,384]{0,1:T(8,128)(2,1)S(1)}, bf16[1536,384]{0,1:T(8,128)(2,1)S(1)}, u32[]{:S(2)}, u32[]{:S(2)}) collective-permute-start(bf16[1536,384]{0,1:T(8,128)(2,1)S(1)} %collective-permute-done.19), channel_id=1, source_target_pairs={{2,0},{3,1},{4,2},{5,3},{10,8},{11,9},{12,10},{13,11},{18,16},{19,... | collective-permute-start | bytes 3538952 | tf_op jit(solution)/shard_map/ppermute | solution.py:43
  139.5 49.1 %copy-start.11 = (bf16[1536,384]{0,1:T(8,128)(2,1)}, bf16[1536,384]{0,1:T(8,128)(2,1)S(1)}, u32[]{:S(2)}) copy-start(bf16[1536,384]{0,1:T(8,128)(2,1)S(1)} %collective-permute-done.17) | copy-start | bytes 3538948
  139.5 49.1 %collective-permute-start.22 = (bf16[1536,384]{0,1:T(8,128)(2,1)S(1)}, bf16[1536,384]{0,1:T(8,128)(2,1)S(1)}, u32[]{:S(2)}, u32[]{:S(2)}) collective-permute-start(bf16[1536,384]{0,1:T(8,128)(2,1)S(1)} %collective-permute-done.17), channel_id=1, source_target_pairs={{0,1},{1,0},{2,3},{3,2},{4,5},{5,4},{6,7},{7,6},{8,9},{9,8},{10,11... | collective-permute-start | bytes 3538952 | tf_op jit(solution)/shard_map/ppermute | solution.py:18
  163.4 25.8 %collective-permute-start.18 = (bf16[1536,384]{0,1:T(8,128)(2,1)S(1)}, bf16[1536,384]{0,1:T(8,128)(2,1)S(1)}, u32[]{:S(2)}, u32[]{:S(2)}) collective-permute-start(bf16[1536,384]{0,1:T(8,128)(2,1)S(1)} %collective-permute-done.17), channel_id=1, source_target_pairs={{2,4},{3,5},{4,6},{5,7},{10,12},{11,13},{12,14},{13,15},{18,20},{1... | collective-permute-start | bytes 3538952 | tf_op jit(solution)/shard_map/ppermute | solution.py:43
  164.1 49.4 %collective-permute-start.10 = (bf16[1536,384]{0,1:T(8,128)(2,1)}, bf16[1536,384]{0,1:T(8,128)(2,1)}, u32[]{:S(2)}, u32[]{:S(2)}) collective-permute-start(bf16[1536,384]{0,1:T(8,128)(2,1)} %collective-permute-done.9), channel_id=1, source_target_pairs={{2,0},{3,1},{4,2},{5,3},{10,8},{11,9},{12,10},{13,11},{18,16},{19,... | collective-permute-start | bytes 3538952 | tf_op jit(solution)/shard_map/ppermute | solution.py:43
  165.4 48.1 %collective-permute-start.8 = (bf16[1536,384]{0,1:T(8,128)(2,1)}, bf16[1536,384]{0,1:T(8,128)(2,1)}, u32[]{:S(2)}, u32[]{:S(2)}) collective-permute-start(bf16[1536,384]{0,1:T(8,128)(2,1)} %collective-permute-done.7), channel_id=1, source_target_pairs={{2,4},{3,5},{4,6},{5,7},{10,12},{11,13},{12,14},{13,15},{18,20},{1... | collective-permute-start | bytes 3538952 | tf_op jit(solution)/shard_map/ppermute | solution.py:43
  188.5 28.8 %collective-permute-start.11 = (bf16[1536,384]{0,1:T(8,128)(2,1)}, bf16[1536,384]{0,1:T(8,128)(2,1)}, u32[]{:S(2)}, u32[]{:S(2)}) collective-permute-start(bf16[1536,384]{0,1:T(8,128)(2,1)} %fusion.9), channel_id=1, source_target_pairs={{0,1},{1,0},{2,3},{3,2},{4,5},{5,4},{6,7},{7,6},{8,9},{9,8},{10,11... | collective-permute-start | bytes 3538952 | tf_op jit(solution)/shard_map/ppermute | solution.py:18
  188.6 1.1 copy-start.13
  188.6 29.3 %collective-permute-start.13 = (bf16[1536,384]{0,1:T(8,128)(2,1)}, bf16[1536,384]{0,1:T(8,128)(2,1)S(1)}, u32[]{:S(2)}, u32[]{:S(2)}) collective-permute-start(bf16[1536,384]{0,1:T(8,128)(2,1)} %collective-permute-done.9), channel_id=1, source_target_pairs={{0,1},{1,0},{2,3},{3,2},{4,5},{5,4},{6,7},{7,6},{8,9},{9,8},{10,11... | collective-permute-start | bytes 3538952 | tf_op jit(solution)/shard_map/ppermute | solution.py:18
  189.6 1.0 copy-start.15
  190.6 27.2 %collective-permute-start.12 = (bf16[1536,384]{0,1:T(8,128)(2,1)}, bf16[1536,384]{0,1:T(8,128)(2,1)}, u32[]{:S(2)}, u32[]{:S(2)}) collective-permute-start(bf16[1536,384]{0,1:T(8,128)(2,1)} %collective-permute-done.7), channel_id=1, source_target_pairs={{0,1},{1,0},{2,3},{3,2},{4,5},{5,4},{6,7},{7,6},{8,9},{9,8},{10,11... | collective-permute-start | bytes 3538952 | tf_op jit(solution)/shard_map/ppermute | solution.py:18
  213.5 17.8 %collective-permute-start.25 = (bf16[1536,384]{0,1:T(8,128)(2,1)}, bf16[1536,384]{0,1:T(8,128)(2,1)}, u32[]{:S(2)}, u32[]{:S(2)}) collective-permute-start(bf16[1536,384]{0,1:T(8,128)(2,1)} %broadcast_select_fusion), channel_id=1, source_target_pairs={{0,1},{1,0},{2,3},{3,2},{4,5},{5,4},{6,7},{7,6},{8,9},{9,8},{10,11... | collective-permute-start | bytes 3538952 | tf_op jit(solution)/shard_map/ppermute | solution.py:18
  213.5 33.3 %collective-permute-start.24 = (bf16[1536,384]{0,1:T(8,128)(2,1)}, bf16[1536,384]{0,1:T(8,128)(2,1)}, u32[]{:S(2)}, u32[]{:S(2)}) collective-permute-start(bf16[1536,384]{0,1:T(8,128)(2,1)} %broadcast_select_fusion), channel_id=1, source_target_pairs={{4,6},{5,7},{2,0},{3,1},{12,14},{13,15},{10,8},{11,9},{20,22},{21,... | collective-permute-start | bytes 3538952 | tf_op jit(solution)/shard_map/ppermute | solution.py:43
  214.8 10.1 %copy-start.10 = (bf16[1536,384]{0,1:T(8,128)(2,1)S(1)}, bf16[1536,384]{0,1:T(8,128)(2,1)}, u32[]{:S(2)}) copy-start(bf16[1536,384]{0,1:T(8,128)(2,1)} %copy-done.9) | copy-start | bytes 3538948
  217.3 35.7 %collective-permute-start.15 = (bf16[1536,384]{0,1:T(8,128)(2,1)}, bf16[1536,384]{0,1:T(8,128)(2,1)}, u32[]{:S(2)}, u32[]{:S(2)}) collective-permute-start(bf16[1536,384]{0,1:T(8,128)(2,1)} %broadcast_select_fusion.1), channel_id=1, source_target_pairs={{0,1},{1,0},{2,3},{3,2},{4,5},{5,4},{6,7},{7,6},{8,9},{9,8},{10,11... | collective-permute-start | bytes 3538952 | tf_op jit(solution)/shard_map/ppermute | solution.py:18
  217.9 52.3 %collective-permute-start.14 = (bf16[1536,384]{0,1:T(8,128)(2,1)}, bf16[1536,384]{0,1:T(8,128)(2,1)}, u32[]{:S(2)}, u32[]{:S(2)}) collective-permute-start(bf16[1536,384]{0,1:T(8,128)(2,1)} %broadcast_select_fusion.1), channel_id=1, source_target_pairs={{4,6},{5,7},{2,0},{3,1},{12,14},{13,15},{10,8},{11,9},{20,22},{21,... | collective-permute-start | bytes 3538952 | tf_op jit(solution)/shard_map/ppermute | solution.py:43
  219.4 7.7 %copy-start = (bf16[384,12288]{1,0:T(8,128)(2,1)S(1)}, bf16[384,12288]{1,0:T(8,128)(2,1)}, u32[]{:S(2)}) copy-start(bf16[384,12288]{1,0:T(8,128)(2,1)} %all-gather.5.cloned.1.call-done) | copy-start | bytes 28311556
  227.0 2.2 copy-start.12
  229.2 1.3 copy-start.14
  246.8 28.2 %collective-permute-start.26 = (bf16[1536,384]{0,1:T(8,128)(2,1)}, bf16[1536,384]{0,1:T(8,128)(2,1)}, u32[]{:S(2)}, u32[]{:S(2)}) collective-permute-start(bf16[1536,384]{0,1:T(8,128)(2,1)} %collective-permute-done.24), channel_id=1, source_target_pairs={{0,1},{1,0},{2,3},{3,2},{4,5},{5,4},{6,7},{7,6},{8,9},{9,8},{10,11... | collective-permute-start | bytes 3538952 | tf_op jit(solution)/shard_map/ppermute | solution.py:18
  270.2 7.4 %collective-permute-start.16 = (bf16[1536,384]{0,1:T(8,128)(2,1)}, bf16[1536,384]{0,1:T(8,128)(2,1)S(1)}, u32[]{:S(2)}, u32[]{:S(2)}) collective-permute-start(bf16[1536,384]{0,1:T(8,128)(2,1)} %collective-permute-done.14), channel_id=1, source_target_pairs={{0,1},{1,0},{2,3},{3,2},{4,5},{5,4},{6,7},{7,6},{8,9},{9,8},{10,11... | collective-permute-start | bytes 3538952 | tf_op jit(solution)/shard_map/ppermute | solution.py:18
  277.5 2.3 copy-start.5
  277.5 2.3 copy-start.8
  277.5 2.3 copy-start.16
  277.5 2.3 copy-start.17
Sparse Core Ops, SparseCore 0:
  20.7 53.2 all-gather.2
  102.4 96.6 all-gather.4

commit v5 on v4

--- a/solution.py
+++ b/solution.py
@@ -92,7 +92,8 @@
     normed_all = lax.all_gather(normed, "col", axis=0, tiled=True)
 
     tokens = state.shape[1]
-    spans = [(0, tokens // 2), (tokens // 2, tokens)]
+    cut = tokens * 2 // 3 if tokens % 384 == 0 else tokens // 2
+    spans = [(0, cut), (cut, tokens)]
     chains = []
     for lo, hi in spans:
         pre_act = None

time: 290 us -> 325 us (1.12)
  waiting for transfers between devices: 159 us -> 190 us
  starting transfers between devices: 35.7 us -> 40.4 us
    ppermute x10, waiting for transfers between devices: 92.2 us -> 123 us  [chain_step(): lax.ppermute(value, 'col', [(2 * a + core, 2 * b + core) for a, b in move...]
    ppermute x10, starting transfers between devices: 20.5 us -> 25.5 us  [chain_step(): lax.ppermute(value, 'col', [(2 * a + core, 2 * b + core) for a, b in move...]
  transfers between devices with their start and end apart: 29 -> 29, of which waited for: 13 -> 11; matrix products, arithmetic and copies ran while one was open for 24% -> 21% of each run, Pallas kernels for 0% -> 0%
where the time goes in v5:
time: 325 us; the launch traced here: 324 us
  waiting for transfers between devices  190 us (58%)
  matrix products  65.3 us (20%)
  starting transfers between devices  40.4 us (12%)
  between operations  14.6 us (4%)
  other arithmetic  8.37 us (3%)
  local copies, waits for them, and re-layouts  4.49 us (1%)
    ppermute x10, waiting for transfers between devices, chain_step(): lax.ppermute(value, 'col', [(2 * a + core, 2 * b + core) for a, b in move...  123 us
    ppermute x17, waiting for transfers between devices, flipped(): return lax.ppermute(value, axis, [(i, i ^ bits) for i in range(devices)])  67.5 us
    dot_general x20, matrix products, on_device(): term = jnp.dot(weights, value, preferred_element_type=jnp.float32)  37.3 us
    dot_general x10, matrix products, on_device(): lax.dot_general(piece, part, (((0,), (0,)), ((), ())), preferred_element_...  28 us
    ppermute x10, starting transfers between devices, chain_step(): lax.ppermute(value, 'col', [(2 * a + core, 2 * b + core) for a, b in move...  25.5 us
    ppermute x17, starting transfers between devices, flipped(): return lax.ppermute(value, axis, [(i, i ^ bits) for i in range(devices)])  14.8 us
  transfers between devices with their start and end apart: 29, of which 11 were waited for; matrix products, arithmetic and copies ran while one was open for 21% of the time, Pallas kernels for 0%

profile of v5, /device:TPU:0, one launch (start us, length us, event | category | flops | bytes accessed | tf_op | source)
XLA Modules:
  0.0 323.5 jit_solution(1059737302696078388)
XLA Ops:
  7.2 1.5 fusion.115
  9.3 0.8 collective-permute-done
  10.1 3.0 collective-permute-start.1
  13.1 1.6 collective-permute-done.1
  14.7 3.1 collective-permute-start.2
  17.8 0.7 broadcast_add_fusion
  18.5 0.9 collective-permute-done.2
  19.5 1.7 add_convert_fusion
  21.3 1.9 collective-permute-start.3
  23.1 1.5 collective-permute-start.4
  24.7 48.2 %collective-permute-done.3 = bf16[768,1536]{1,0:T(8,128)(2,1)S(1)} collective-permute-done((bf16[768,1536]{1,0:T(8,128)(2,1)}, bf16[768,1536]{1,0:T(8,128)(2,1)S(1)}, u32[]{:S(2)}, u32[]{:S(2)}) %collective-permute-start.3) | collective-permute-done | bytes 2359328 | tf_op jit(solution)/shard_map/ppermute | solution.py:18
  72.8 1.1 slice.19
  73.9 1.6 collective-permute-start.6
  75.5 1.4 copy-done.1
  76.9 1.1 slice.18
  78.0 1.5 collective-permute-start.5
  79.5 2.6 fusion.64
  82.1 1.9 convolution_add_fusion.3
  84.0 3.0 fusion.9
  87.0 12.5 %collective-permute-done.6 = bf16[384,1536]{1,0:T(8,128)(2,1)} collective-permute-done((bf16[384,1536]{1,0:T(8,128)(2,1)}, bf16[384,1536]{1,0:T(8,128)(2,1)}, u32[]{:S(2)}, u32[]{:S(2)}) %collective-permute-start.6) | collective-permute-done | bytes 1179680 | tf_op jit(solution)/shard_map/ppermute | solution.py:18
  99.5 3.5 %collective-permute-done.5 = bf16[384,1536]{1,0:T(8,128)(2,1)} collective-permute-done((bf16[384,1536]{1,0:T(8,128)(2,1)}, bf16[384,1536]{1,0:T(8,128)(2,1)}, u32[]{:S(2)}, u32[]{:S(2)}) %collective-permute-start.5) | collective-permute-done | bytes 1179680 | tf_op jit(solution)/shard_map/ppermute | solution.py:18
  103.0 3.3 %fusion.60 = f32[512,1536]{1,0:T(8,128)S(1)} fusion(bf16[768,1536]{1,0:T(8,128)(2,1)} %param.14, bf16[3072,768]{1,0:T(8,128)(2,1)} %all-gather.3.cloned.1.call-done, s32[]{:T(128)S(6)} %select_n.98), kind=kOutput, calls=%fused_computation.80 | convolution fusion | flops 1207959552 | bytes 6291460 | tf_op jit(solution)/shard_map/dot_general | solution.py:107
  106.3 2.8 convolution_add_fusion.1
  109.1 2.7 fusion
  111.9 2.6 fusion.70
  114.5 4.8 %fusion.8 = bf16[1536,512]{0,1:T(8,128)(2,1)} fusion(f32[1536,512]{0,1:T(8,128)S(1)} %fusion, f32[1536,512]{0,1:T(8,128)S(1)} %fusion.70, f32[1536]{0:T(1024)S(1)} %copy-done.14, bf16[384,1536]{1,0:T(8,128)(2,1)} %collective-permute-done.6, bf16[3072,768]{1,0:T(8,128)(2,1)} %all-gather.3.cloned.1.call-done, s32[]{:T(128)S(6)} %select_n.102), kind=kOutput, calls=%fused_computation.11 | convolution fusion | flops 613416960 | bytes 9443332 | tf_op jit(solution)/shard_map/dot_general | solution.py:107
  119.3 1.4 collective-permute-start.9
  120.7 5.7 %collective-permute-start.7 = (bf16[1536,512]{0,1:T(8,128)(2,1)}, bf16[1536,512]{0,1:T(8,128)(2,1)}, u32[]{:S(2)}, u32[]{:S(2)}) collective-permute-start(bf16[1536,512]{0,1:T(8,128)(2,1)} %fusion.8), channel_id=1, source_target_pairs={{0,2},{1,3},{2,4},{3,5},{4,6},{5,7},{8,10},{9,11},{10,12},{11,13},... | collective-permute-start | bytes 4718600 | tf_op jit(solution)/shard_map/ppermute | solution.py:43
  126.4 1.9 fusion.76
  128.3 2.3 fusion.17
  130.7 1.3 collective-permute-start.19
  132.1 26.9 %collective-permute-done.9 = bf16[1536,512]{0,1:T(8,128)(2,1)} collective-permute-done((bf16[1536,512]{0,1:T(8,128)(2,1)}, bf16[1536,512]{0,1:T(8,128)(2,1)}, u32[]{:S(2)}, u32[]{:S(2)}) %collective-permute-start.9) | collective-permute-done | bytes 1572896 | tf_op jit(solution)/shard_map/ppermute | solution.py:43
  159.0 1.3 collective-permute-start.10
  160.3 1.8 collective-permute-start.8
  162.1 8.4 %collective-permute-start.17 = (bf16[1536,256]{0,1:T(8,128)(2,1)S(1)}, bf16[1536,256]{0,1:T(8,128)(2,1)}, u32[]{:S(2)}, u32[]{:S(2)}) collective-permute-start(bf16[1536,256]{0,1:T(8,128)(2,1)S(1)} %fusion.17), channel_id=1, source_target_pairs={{0,2},{1,3},{2,4},{3,5},{4,6},{5,7},{8,10},{9,11},{10,12},{11,13},... | collective-permute-start | bytes 2359304 | tf_op jit(solution)/shard_map/ppermute | solution.py:43
  170.5 5.2 %collective-permute-done.19 = bf16[1536,256]{0,1:T(8,128)(2,1)S(1)} collective-permute-done((bf16[1536,256]{0,1:T(8,128)(2,1)S(1)}, bf16[1536,256]{0,1:T(8,128)(2,1)S(1)}, u32[]{:S(2)}, u32[]{:S(2)}) %collective-permute-start.19) | collective-permute-done | bytes 786464 | tf_op jit(solution)/shard_map/ppermute | solution.py:43
  175.7 1.5 collective-permute-start.20
  177.2 1.9 collective-permute-done.17
  179.6 41.2 %collective-permute-done.20 = bf16[1536,256]{0,1:T(8,128)(2,1)S(1)} collective-permute-done((bf16[1536,256]{0,1:T(8,128)(2,1)S(1)}, bf16[1536,256]{0,1:T(8,128)(2,1)S(1)}, u32[]{:S(2)}, u32[]{:S(2)}) %collective-permute-start.20) | collective-permute-done | bytes 786464 | tf_op jit(solution)/shard_map/ppermute | solution.py:43
  220.8 0.8 copy-done.9
  221.7 1.5 collective-permute-start.18
  223.2 1.3 broadcast_select_fusion
  225.1 1.2 broadcast_select_fusion.1
  226.4 1.3 collective-permute-start.24
  227.7 1.3 collective-permute-start.14
  229.1 2.7 fusion.56
  231.8 3.1 fusion.46
  235.0 2.6 fusion.40
  237.6 2.2 fusion.36
  239.8 2.2 convolution_add_fusion.7
  242.0 2.2 convolution_add_fusion.6
  244.2 2.2 fusion.18
  246.5 2.3 fusion.20
  248.8 47.6 %collective-permute-done.14 = bf16[1536,512]{0,1:T(8,128)(2,1)} collective-permute-done((bf16[1536,512]{0,1:T(8,128)(2,1)}, bf16[1536,512]{0,1:T(8,128)(2,1)}, u32[]{:S(2)}, u32[]{:S(2)}) %collective-permute-start.14) | collective-permute-done | bytes 1572896 | tf_op jit(solution)/shard_map/ppermute | solution.py:43
  296.9 1.6 convolution_add_fusion.11
  298.6 1.6 convolution_add_fusion.10
  300.7 1.6 fusion.22
  302.9 1.7 fusion.34
  305.1 0.6 collective-permute-start.26
  305.7 2.0 fusion.30
  307.7 2.6 fusion.32
  310.3 1.8 add_add_fusion.1
  312.1 2.7 add_add_fusion
  314.8 1.8 multiply_add_fusion
  (71 shorter events, 4.0 us)
Async XLA Ops:
  7.2 12.3 %copy-start.4 = (f32[384,768]{1,0:T(8,128)S(1)}, f32[384,768]{1,0:T(8,128)}, u32[]{:S(2)}) copy-start(f32[384,768]{1,0:T(8,128)} %param.9) | copy-start | bytes 3538948
  7.2 72.3 %all-gather.3.cloned.1.call-start = ((), (), s32[]{:S(2)}) async-start(), calls=%async_computation | async-start | bytes 5308416 | tf_op jit(solution)/shard_map/all_gather | solution.py:92
  8.8 1.3 collective-permute-start
  10.1 4.6 %collective-permute-start.1 = (f32[2,768]{1,0:T(2,128)S(1)}, f32[2,768]{1,0:T(2,128)S(1)}, u32[]{:S(2)}, u32[]{:S(2)}) collective-permute-start(f32[2,768]{1,0:T(2,128)S(1)} %fusion.114), channel_id=1, source_target_pairs={{0,2},{1,3},{2,0},{3,1},{4,6},{5,7},{6,4},{7,5},{8,10},{9,11},{10,... | collective-permute-start | bytes 18440 | tf_op jit(solution)/shard_map/ppermute | solution.py:18
  14.7 4.7 %collective-permute-start.2 = (f32[2,768]{1,0:T(2,128)S(1)}, f32[2,768]{1,0:T(2,128)S(1)}, u32[]{:S(2)}, u32[]{:S(2)}) collective-permute-start(f32[2,768]{1,0:T(2,128)S(1)} %fusion.147), channel_id=1, source_target_pairs={{0,4},{1,5},{2,6},{3,7},{4,0},{5,1},{6,2},{7,3},{8,12},{9,13},{10,... | collective-permute-start | bytes 18440 | tf_op jit(solution)/shard_map/ppermute | solution.py:18
  21.2 207.9 %all-gather.5.cloned.1.call-start = ((), (), s32[]{:S(2)}) async-start(), calls=%async_computation.1 | async-start | bytes 11796480 | tf_op jit(solution)/shard_map/all_gather | solution.py:114
  21.3 51.6 %collective-permute-start.3 = (bf16[768,1536]{1,0:T(8,128)(2,1)}, bf16[768,1536]{1,0:T(8,128)(2,1)S(1)}, u32[]{:S(2)}, u32[]{:S(2)}) collective-permute-start(bf16[768,1536]{1,0:T(8,128)(2,1)} %param.14), channel_id=1, source_target_pairs={{0,8},{8,0},{16,24},{24,16},{1,9},{9,1},{17,25},{25,17},{2,10},{10... | collective-permute-start | bytes 7077896 | tf_op jit(solution)/shard_map/ppermute | solution.py:18
  23.1 52.4 %collective-permute-start.4 = (bf16[768,1536]{1,0:T(8,128)(2,1)}, bf16[768,1536]{1,0:T(8,128)(2,1)S(1)}, u32[]{:S(2)}, u32[]{:S(2)}) collective-permute-start(bf16[768,1536]{1,0:T(8,128)(2,1)} %param.14), channel_id=1, source_target_pairs={{0,16},{8,24},{16,0},{24,8},{1,17},{9,25},{17,1},{25,9},{2,18},{10... | collective-permute-start | bytes 7077896 | tf_op jit(solution)/shard_map/ppermute | solution.py:18
  73.9 25.6 %collective-permute-start.6 = (bf16[384,1536]{1,0:T(8,128)(2,1)}, bf16[384,1536]{1,0:T(8,128)(2,1)}, u32[]{:S(2)}, u32[]{:S(2)}) collective-permute-start(bf16[384,1536]{1,0:T(8,128)(2,1)} %slice.19), channel_id=1, source_target_pairs={{0,16},{8,24},{16,0},{24,8},{1,17},{9,25},{17,1},{25,9},{2,18},{10... | collective-permute-start | bytes 3538952 | tf_op jit(solution)/shard_map/ppermute | solution.py:18
  75.5 1.4 copy-start.1
  78.0 25.0 %collective-permute-start.5 = (bf16[384,1536]{1,0:T(8,128)(2,1)}, bf16[384,1536]{1,0:T(8,128)(2,1)}, u32[]{:S(2)}, u32[]{:S(2)}) collective-permute-start(bf16[384,1536]{1,0:T(8,128)(2,1)} %slice.18), channel_id=1, source_target_pairs={{0,8},{8,0},{16,24},{24,16},{1,9},{9,1},{17,25},{25,17},{2,10},{10... | collective-permute-start | bytes 3538952 | tf_op jit(solution)/shard_map/ppermute | solution.py:18
  82.1 2.0 copy-start.2
  106.3 2.8 copy-start.3
  111.8 2.6 copy-start.14
  119.3 9.0 %copy-start.5 = (f32[1536,256]{0,1:T(8,128)S(1)}, f32[1536,256]{0,1:T(8,128)}, u32[]{:S(2)}) copy-start(f32[1536,256]{0,1:T(8,128)} %fusion.9) | copy-start | bytes 4718596
  119.3 39.7 %collective-permute-start.9 = (bf16[1536,512]{0,1:T(8,128)(2,1)}, bf16[1536,512]{0,1:T(8,128)(2,1)}, u32[]{:S(2)}, u32[]{:S(2)}) collective-permute-start(bf16[1536,512]{0,1:T(8,128)(2,1)} %fusion.8), channel_id=1, source_target_pairs={{2,0},{3,1},{4,2},{5,3},{6,4},{7,5},{10,8},{11,9},{12,10},{13,11},... | collective-permute-start | bytes 4718600 | tf_op jit(solution)/shard_map/ppermute | solution.py:43
  120.7 39.5 %collective-permute-start.7 = (bf16[1536,512]{0,1:T(8,128)(2,1)}, bf16[1536,512]{0,1:T(8,128)(2,1)}, u32[]{:S(2)}, u32[]{:S(2)}) collective-permute-start(bf16[1536,512]{0,1:T(8,128)(2,1)} %fusion.8), channel_id=1, source_target_pairs={{0,2},{1,3},{2,4},{3,5},{4,6},{5,7},{8,10},{9,11},{10,12},{11,13},... | collective-permute-start | bytes 4718600 | tf_op jit(solution)/shard_map/ppermute | solution.py:43
  130.7 90.1 %copy-start.7 = (bf16[1536,256]{0,1:T(8,128)(2,1)}, bf16[1536,256]{0,1:T(8,128)(2,1)S(1)}, u32[]{:S(2)}) copy-start(bf16[1536,256]{0,1:T(8,128)(2,1)S(1)} %fusion.17) | copy-start | bytes 2359300
  130.7 45.0 %collective-permute-start.19 = (bf16[1536,256]{0,1:T(8,128)(2,1)S(1)}, bf16[1536,256]{0,1:T(8,128)(2,1)S(1)}, u32[]{:S(2)}, u32[]{:S(2)}) collective-permute-start(bf16[1536,256]{0,1:T(8,128)(2,1)S(1)} %fusion.17), channel_id=1, source_target_pairs={{2,0},{3,1},{4,2},{5,3},{6,4},{7,5},{10,8},{11,9},{12,10},{13,11},... | collective-permute-start | bytes 2359304 | tf_op jit(solution)/shard_map/ppermute | solution.py:43
  132.0 43.7 %collective-permute-start.21 = (bf16[1536,256]{0,1:T(8,128)(2,1)S(1)}, bf16[1536,256]{0,1:T(8,128)(2,1)}, u32[]{:S(2)}, u32[]{:S(2)}) collective-permute-start(bf16[1536,256]{0,1:T(8,128)(2,1)S(1)} %fusion.17), channel_id=1, source_target_pairs={{0,1},{1,0},{2,3},{3,2},{4,5},{5,4},{6,7},{7,6},{8,9},{9,8},{10,11... | collective-permute-start | bytes 2359304 | tf_op jit(solution)/shard_map/ppermute | solution.py:18
  159.0 61.9 %collective-permute-start.10 = (bf16[1536,512]{0,1:T(8,128)(2,1)}, bf16[1536,512]{0,1:T(8,128)(2,1)S(1)}, u32[]{:S(2)}, u32[]{:S(2)}) collective-permute-start(bf16[1536,512]{0,1:T(8,128)(2,1)} %collective-permute-done.9), channel_id=1, source_target_pairs={{2,0},{3,1},{4,2},{5,3},{10,8},{11,9},{12,10},{13,11},{18,16},{19,... | collective-permute-start | bytes 4718600 | tf_op jit(solution)/shard_map/ppermute | solution.py:43
  160.3 63.0 %collective-permute-start.8 = (bf16[1536,512]{0,1:T(8,128)(2,1)}, bf16[1536,512]{0,1:T(8,128)(2,1)}, u32[]{:S(2)}, u32[]{:S(2)}) collective-permute-start(bf16[1536,512]{0,1:T(8,128)(2,1)} %collective-permute-done.7), channel_id=1, source_target_pairs={{2,4},{3,5},{4,6},{5,7},{10,12},{11,13},{12,14},{13,15},{18,20},{1... | collective-permute-start | bytes 4718600 | tf_op jit(solution)/shard_map/ppermute | solution.py:43
  162.1 17.0 %collective-permute-start.17 = (bf16[1536,256]{0,1:T(8,128)(2,1)S(1)}, bf16[1536,256]{0,1:T(8,128)(2,1)}, u32[]{:S(2)}, u32[]{:S(2)}) collective-permute-start(bf16[1536,256]{0,1:T(8,128)(2,1)S(1)} %fusion.17), channel_id=1, source_target_pairs={{0,2},{1,3},{2,4},{3,5},{4,6},{5,7},{8,10},{9,11},{10,12},{11,13},... | collective-permute-start | bytes 2359304 | tf_op jit(solution)/shard_map/ppermute | solution.py:43
  175.7 3.4 %collective-permute-start.23 = (bf16[1536,256]{0,1:T(8,128)(2,1)S(1)}, bf16[1536,256]{0,1:T(8,128)(2,1)S(1)}, u32[]{:S(2)}, u32[]{:S(2)}) collective-permute-start(bf16[1536,256]{0,1:T(8,128)(2,1)S(1)} %collective-permute-done.19), channel_id=1, source_target_pairs={{0,1},{1,0},{2,3},{3,2},{4,5},{5,4},{6,7},{7,6},{8,9},{9,8},{10,11... | collective-permute-start | bytes 2359304 | tf_op jit(solution)/shard_map/ppermute | solution.py:18
  175.7 45.1 %collective-permute-start.20 = (bf16[1536,256]{0,1:T(8,128)(2,1)S(1)}, bf16[1536,256]{0,1:T(8,128)(2,1)S(1)}, u32[]{:S(2)}, u32[]{:S(2)}) collective-permute-start(bf16[1536,256]{0,1:T(8,128)(2,1)S(1)} %collective-permute-done.19), channel_id=1, source_target_pairs={{2,0},{3,1},{4,2},{5,3},{10,8},{11,9},{12,10},{13,11},{18,16},{19,... | collective-permute-start | bytes 2359304 | tf_op jit(solution)/shard_map/ppermute | solution.py:43
  179.1 47.3 %collective-permute-start.11 = (bf16[1536,512]{0,1:T(8,128)(2,1)}, bf16[1536,512]{0,1:T(8,128)(2,1)}, u32[]{:S(2)}, u32[]{:S(2)}) collective-permute-start(bf16[1536,512]{0,1:T(8,128)(2,1)} %fusion.8), channel_id=1, source_target_pairs={{0,1},{1,0},{2,3},{3,2},{4,5},{5,4},{6,7},{7,6},{8,9},{9,8},{10,11... | collective-permute-start | bytes 4718600 | tf_op jit(solution)/shard_map/ppermute | solution.py:18
  179.1 41.8 %copy-start.10 = (bf16[1536,256]{0,1:T(8,128)(2,1)}, bf16[1536,256]{0,1:T(8,128)(2,1)S(1)}, u32[]{:S(2)}) copy-start(bf16[1536,256]{0,1:T(8,128)(2,1)S(1)} %collective-permute-done.23) | copy-start | bytes 2359300
  179.1 48.6 %collective-permute-start.13 = (bf16[1536,512]{0,1:T(8,128)(2,1)}, bf16[1536,512]{0,1:T(8,128)(2,1)}, u32[]{:S(2)}, u32[]{:S(2)}) collective-permute-start(bf16[1536,512]{0,1:T(8,128)(2,1)} %collective-permute-done.9), channel_id=1, source_target_pairs={{0,1},{1,0},{2,3},{3,2},{4,5},{5,4},{6,7},{7,6},{8,9},{9,8},{10,11... | collective-permute-start | bytes 4718600 | tf_op jit(solution)/shard_map/ppermute | solution.py:18
  220.8 0.9 copy-start.9
  220.8 6.9 %collective-permute-start.12 = (bf16[1536,512]{0,1:T(8,128)(2,1)}, bf16[1536,512]{0,1:T(8,128)(2,1)}, u32[]{:S(2)}, u32[]{:S(2)}) collective-permute-start(bf16[1536,512]{0,1:T(8,128)(2,1)} %collective-permute-done.7), channel_id=1, source_target_pairs={{0,1},{1,0},{2,3},{3,2},{4,5},{5,4},{6,7},{7,6},{8,9},{9,8},{10,11... | collective-permute-start | bytes 4718600 | tf_op jit(solution)/shard_map/ppermute | solution.py:18
  221.7 2.9 collective-permute-start.18
  223.2 3.1 collective-permute-start.22
  224.6 13.0 %collective-permute-start.15 = (bf16[1536,512]{0,1:T(8,128)(2,1)}, bf16[1536,512]{0,1:T(8,128)(2,1)}, u32[]{:S(2)}, u32[]{:S(2)}) collective-permute-start(bf16[1536,512]{0,1:T(8,128)(2,1)} %broadcast_select_fusion), channel_id=1, source_target_pairs={{0,1},{1,0},{2,3},{3,2},{4,5},{5,4},{6,7},{7,6},{8,9},{9,8},{10,11... | collective-permute-start | bytes 4718600 | tf_op jit(solution)/shard_map/ppermute | solution.py:18
  226.3 76.5 %collective-permute-start.25 = (bf16[1536,256]{0,1:T(8,128)(2,1)S(1)}, bf16[1536,256]{0,1:T(8,128)(2,1)}, u32[]{:S(2)}, u32[]{:S(2)}) collective-permute-start(bf16[1536,256]{0,1:T(8,128)(2,1)S(1)} %broadcast_select_fusion.1), channel_id=1, source_target_pairs={{0,1},{1,0},{2,3},{3,2},{4,5},{5,4},{6,7},{7,6},{8,9},{9,8},{10,11... | collective-permute-start | bytes 2359304 | tf_op jit(solution)/shard_map/ppermute | solution.py:18
  226.4 78.7 %collective-permute-start.24 = (bf16[1536,256]{0,1:T(8,128)(2,1)S(1)}, bf16[1536,256]{0,1:T(8,128)(2,1)}, u32[]{:S(2)}, u32[]{:S(2)}) collective-permute-start(bf16[1536,256]{0,1:T(8,128)(2,1)S(1)} %broadcast_select_fusion.1), channel_id=1, source_target_pairs={{4,6},{5,7},{2,0},{3,1},{12,14},{13,15},{10,8},{11,9},{20,22},{21,... | collective-permute-start | bytes 2359304 | tf_op jit(solution)/shard_map/ppermute | solution.py:43
  227.7 68.6 %collective-permute-start.14 = (bf16[1536,512]{0,1:T(8,128)(2,1)}, bf16[1536,512]{0,1:T(8,128)(2,1)}, u32[]{:S(2)}, u32[]{:S(2)}) collective-permute-start(bf16[1536,512]{0,1:T(8,128)(2,1)} %broadcast_select_fusion), channel_id=1, source_target_pairs={{4,6},{5,7},{2,0},{3,1},{12,14},{13,15},{10,8},{11,9},{20,22},{21,... | collective-permute-start | bytes 4718600 | tf_op jit(solution)/shard_map/ppermute | solution.py:43
  229.1 8.5 %copy-start = (bf16[384,12288]{1,0:T(8,128)(2,1)S(1)}, bf16[384,12288]{1,0:T(8,128)(2,1)}, u32[]{:S(2)}) copy-start(bf16[384,12288]{1,0:T(8,128)(2,1)} %all-gather.5.cloned.1.call-done) | copy-start | bytes 28311556
  246.5 49.9 %copy-start.8 = (bf16[1536,256]{0,1:T(8,128)(2,1)S(1)}, bf16[1536,256]{0,1:T(8,128)(2,1)}, u32[]{:S(2)}) copy-start(bf16[1536,256]{0,1:T(8,128)(2,1)} %copy-done.7) | copy-start | bytes 2359300
  296.4 15.7 %collective-permute-start.16 = (bf16[1536,512]{0,1:T(8,128)(2,1)}, bf16[1536,512]{0,1:T(8,128)(2,1)}, u32[]{:S(2)}, u32[]{:S(2)}) collective-permute-start(bf16[1536,512]{0,1:T(8,128)(2,1)} %collective-permute-done.14), channel_id=1, source_target_pairs={{0,1},{1,0},{2,3},{3,2},{4,5},{5,4},{6,7},{7,6},{8,9},{9,8},{10,11... | collective-permute-start | bytes 4718600 | tf_op jit(solution)/shard_map/ppermute | solution.py:18
  302.9 1.7 copy-start.11
  305.1 5.2 %collective-permute-start.26 = (bf16[1536,256]{0,1:T(8,128)(2,1)}, bf16[1536,256]{0,1:T(8,128)(2,1)S(1)}, u32[]{:S(2)}, u32[]{:S(2)}) collective-permute-start(bf16[1536,256]{0,1:T(8,128)(2,1)} %collective-permute-done.24), channel_id=1, source_target_pairs={{0,1},{1,0},{2,3},{3,2},{4,5},{5,4},{6,7},{7,6},{8,9},{9,8},{10,11... | collective-permute-start | bytes 2359304 | tf_op jit(solution)/shard_map/ppermute | solution.py:18
  312.1 2.7 copy-start.6
  312.1 2.7 copy-start.12
  312.1 2.7 copy-start.13
Sparse Core Ops, SparseCore 0:
  21.3 53.2 all-gather.2
  103.1 96.6 all-gather.4
